TPU v7x, 256 devices: a whole 4x4x8 slice. The times are simulated.
256 devices in a mesh: exp: 64 (over z, x, core), tp: 4 (over y).
Axes of the slice: x: 4, y: 4, z: 8, core: 2. Of those that a mesh axis runs over, the one named last changes fastest.
Arguments:
- tokens: bfloat16 [8192, 3584], P('exp', 'tp'), may hold values from -6 to 6
- expert_ids: int32 [8192, 8], P('exp'), may hold values from 0 to 127, all different within a row; in each aligned block of 128 rows (0 to 127, 128 to 255, ...) at most 10 rows name the same one
- gate_weights: float32 [8192, 8], P('exp'), may hold values from 0.05 to 0.6
- w_gate: bfloat16 [128, 3584, 1024], P('exp', None, 'tp'), may hold values from -0.09375 to 0.09375
- w_up: bfloat16 [128, 3584, 1024], P('exp', None, 'tp'), may hold values from -0.09375 to 0.09375
- w_down: bfloat16 [128, 1024, 3584], P('exp', 'tp'), may hold values from -0.1875 to 0.1875
- s_gate: bfloat16 [3584, 1024], P('exp', 'tp'), may hold values from -0.09375 to 0.09375
- s_up: bfloat16 [3584, 1024], P('exp', 'tp'), may hold values from -0.09375 to 0.09375
- s_down: bfloat16 [1024, 3584], P('tp', 'exp'), may hold values from -0.1875 to 0.1875
Outputs:
- mixed: bfloat16 [8192, 3584], P('exp', 'tp')
Inputs may be any that keep to these rules, and one draw needn't show every extreme that they name: `expert_ids`: each row names 8 different experts. In the 128 rows of one index of exp no expert is named by more than 10 rows, and in every draw some expert is named by exactly 10 rows of some index.
All inputs are finite; a program needn't handle non-finite values.
Results may differ from a plain program's by a relative error of at most 0.015.
Values may be sent and summed in bfloat16 or wider, within the bound.
A program may use at most 128 MiB of HBM per device.

v0:
```python
import jax
import jax.numpy as jnp
from jax import lax
from jax.sharding import PartitionSpec as P


def slot_layout(expert_ids, experts, capacity):
    tok_count = expert_ids.shape[0]
    top_count = expert_ids.shape[1]
    flat_ids = expert_ids.reshape(-1)
    columns = jnp.arange(experts, dtype=jnp.int32)
    onehot = (flat_ids[:, None] == columns[None, :]).astype(jnp.int32)
    position = jnp.sum((jnp.cumsum(onehot, axis=0) - onehot) * onehot, axis=1)
    slot_of = flat_ids * capacity + position
    entries = jnp.arange(tok_count * top_count, dtype=jnp.int32)
    filler = jnp.full((experts * capacity,), -1, jnp.int32).at[slot_of].set(entries)
    present = filler >= 0
    token_of = jnp.where(present, filler // top_count, 0)
    return (slot_of, present, token_of)


def body(tokens, expert_ids, gate_weights, w_gate, w_up, w_down, s_gate, s_up, s_down):
    exp_count = lax.axis_size("exp")
    tok_count = expert_ids.shape[0]
    top_count = expert_ids.shape[1]
    local_experts = w_gate.shape[0]
    width = w_gate.shape[1]
    experts = local_experts * exp_count
    capacity = max(2, 5 * tok_count * top_count // (4 * experts))
    quarter = tokens.shape[1]
    slot_of, present, token_of = slot_layout(expert_ids, experts, capacity)
    whole = lax.all_gather(tokens, "tp", axis=1, tiled=True)
    keep = present[:, None]
    zero_value = jnp.zeros((), tokens.dtype)
    outgoing = jnp.where(keep, whole[token_of], zero_value)
    arrived = lax.all_to_all(
        outgoing.reshape(exp_count, local_experts * capacity, width),
        "exp",
        split_axis=0,
        concat_axis=0,
        tiled=True,
    )
    slot_rows = arrived.reshape(exp_count, local_experts, capacity, width)
    gate = jnp.einsum("secd,edh->sech", slot_rows, w_gate, preferred_element_type=jnp.float32)
    upper = jnp.einsum("secd,edh->sech", slot_rows, w_up, preferred_element_type=jnp.float32)
    hidden = (jax.nn.silu(gate) * upper).astype(jnp.bfloat16)
    partial_out = jnp.einsum("sech,ehd->secd", hidden, w_down, preferred_element_type=jnp.float32)
    rounded = lax.optimization_barrier(partial_out.astype(jnp.bfloat16))
    shared_gate = jnp.dot(
        whole, lax.all_gather(s_gate, "exp", axis=0, tiled=True), preferred_element_type=jnp.float32
    )
    shared_up = jnp.dot(
        whole, lax.all_gather(s_up, "exp", axis=0, tiled=True), preferred_element_type=jnp.float32
    )
    shared_hidden = (jax.nn.silu(shared_gate) * shared_up).astype(jnp.bfloat16)
    shared_part = jnp.dot(
        shared_hidden,
        lax.all_gather(s_down, "exp", axis=1, tiled=True),
        preferred_element_type=jnp.float32,
    )
    weights_flat = gate_weights.reshape(-1)[:, None]
    summed = lax.psum_scatter(
        rounded.astype(jnp.float32).astype(jnp.bfloat16), "tp", scatter_dimension=3, tiled=True
    ).astype(jnp.float32)
    results = summed.reshape(exp_count, local_experts * capacity, quarter)
    homed = lax.all_to_all(
        results.astype(jnp.bfloat16), "exp", split_axis=0, concat_axis=0, tiled=True
    ).astype(results.dtype)
    expert_out = homed.reshape(experts * capacity, quarter)
    picked = expert_out[slot_of] * weights_flat
    routed = jnp.sum(picked.reshape(tok_count, top_count, quarter), axis=1)
    shared_sum = lax.psum_scatter(
        shared_part.astype(jnp.bfloat16), "tp", scatter_dimension=1, tiled=True
    ).astype(jnp.float32)
    total = shared_sum + routed
    return total.astype(jnp.bfloat16)


def solution(mesh):
    return jax.shard_map(
        body,
        mesh=mesh,
        in_specs=(
            P("exp", "tp"),
            P("exp", None),
            P("exp", None),
            P("exp", None, "tp"),
            P("exp", None, "tp"),
            P("exp", "tp", None),
            P("exp", "tp"),
            P("exp", "tp"),
            P("tp", "exp"),
        ),
        out_specs=P("exp", "tp"),
        check_vma=False,
    )
```

profile of v0, /device:TPU:1, one launch (start us, length us, event | category | flops | bytes accessed | tf_op | source)
XLA Modules:
  0.0 708.5 jit_solution(7971309198645339930)
XLA Ops:
  7.4 0.0 copy-start
  7.4 0.0 reduce-scatter.9.cloned.1.call-start
  7.4 0.7 broadcast_multiply_fusion
  8.1 0.8 copy.22
  8.9 0.1 eq.29
  9.0 0.1 eq.25
  9.1 0.1 copy.21
  9.2 0.1 mul.46
  9.3 0.1 copy.24
  9.4 0.2 fusion.29
  9.7 0.1 copy.25
  9.8 0.4 fusion.28
  10.2 4.3 scatter_custom_fusion
  14.5 0.1 broadcast_in_dim.27
  14.7 0.0 copy-done
  14.7 13.9 %all_gather.12 = bf16[128,3584]{1,0:T(8,128)(2,1)S(1)} all-gather(bf16[128,896]{1,0:T(8,128)(2,1)S(1)} %copy-done), channel_id=1, replica_groups=mesh['exp'=64,'tp'=4] {'tp'}, dimensions={1}, use_global_device_ids=true | all-gather | bytes 1146880 | tf_op jit(solution)/shard_map/all_gather | solution.py:32
  28.6 7.8 %gather_fusion = bf16[1280,3584]{1,0:T(8,128)(2,1)} fusion(bf16[128,3584]{1,0:T(8,128)(2,1)S(1)} %all_gather.12, s32[2048]{0:T(1024)S(1)} %pad_clamp_fusion), kind=kCustom, calls=%fused_computation | custom fusion | bytes 18355200 | tf_op jit(solution)/shard_map/gather | solution.py:35
  36.4 13.2 %gather.11 = bf16[64,20,3584]{2,1,0:T(8,128)(2,1)} reshape(bf16[1280,3584]{1,0:T(8,128)(2,1)} %gather_fusion) | data formatting | bytes 18350080 | tf_op jit(solution)/shard_map/gather | solution.py:35
  49.6 5.8 broadcast_select_fusion
  55.3 256.2 %all_to_all.10 = bf16[64,20,3584]{2,1,0:T(8,128)(2,1)} all-to-all(bf16[64,20,3584]{2,1,0:T(8,128)(2,1)S(1)} %broadcast_select_fusion), channel_id=1, replica_groups=mesh['exp'=64,'tp'=4] {'exp'}, dimensions={0} | all-to-all | bytes 18350080 | tf_op jit(solution)/shard_map/all_to_all | solution.py:36
  311.5 10.4 %copy.26 = bf16[64,20,3584]{2,0,1:T(8,128)(2,1)} copy(bf16[64,20,3584]{2,1,0:T(8,128)(2,1)} %all_to_all.10) | data formatting | bytes 18350080 | tf_op jit(solution)/shard_map/all_to_all | solution.py:36
  321.9 7.2 %fusion.6 = f32[64,2,10,256]{3,0,2,1:T(8,128)S(1)} fusion(bf16[64,2,10,3584]{3,0,2,1:T(8,128)(2,1)} %bitcast.70, bf16[2,3584,256]{2,1,0:T(8,128)(2,1)} %param.12), kind=kOutput, calls=%fused_computation.13 | convolution fusion | flops 2348810240 | bytes 14155776 | tf_op jit(solution)/shard_map/secd,edh->sech/dot_general | solution.py:44
  329.1 14.4 %convert_bitcast_fusion = bf16[64,2,10,3584]{3,0,2,1:T(8,128)(2,1)} fusion(bf16[2,256,3584]{2,1,0:T(8,128)(2,1)} %param.14, bf16[64,2,10,3584]{3,0,2,1:T(8,128)(2,1)} %bitcast.71, bf16[2,3584,256]{2,1,0:T(8,128)(2,1)} %param.13, f32[64,2,10,256]{3,0,2,1:T(8,128)S(1)} %fusion.6), kind=kOutput, calls=%fused_computation.4 | convolution fusion | flops 4704174080 | bytes 27000832 | tf_op jit(solution)/shard_map/sech,ehd->secd/dot_general | solution.py:47
  343.5 39.9 %copy.34 = bf16[64,2,10,3584]{0,2,1,3:T(8,128)(2,1)} copy(bf16[64,2,10,3584]{3,0,2,1:T(8,128)(2,1)} %convert_bitcast_fusion) | data formatting | bytes 18350080
  383.3 34.0 %reshape.109 = bf16[3584,1280]{1,0:T(8,128)(2,1)} reshape(bf16[3584,2,10,64]{3,2,1,0:T(8,128)(2,1)} %bitcast.68) | data formatting | bytes 18350080
  417.3 0.0 reduce-scatter.9.cloned.1.call-update
  417.4 0.0 all-gather.4.cloned.1.call-start
  417.4 0.5 all-gather.4.cloned.1.call-update
  417.9 0.0 all-gather.6.cloned.1.call-start
  418.0 0.5 all-gather.6.cloned.1.call-update
  418.5 0.3 all-gather.8.cloned.1.call-start
  418.8 0.3 all-gather.8.cloned.1.call-update
  419.1 84.3 %reduce-scatter.9.cloned.1.call-done = bf16[896,1280]{1,0:T(8,128)(2,1)} async-done(((bf16[3584,1280]{1,0:T(8,128)(2,1)}), bf16[896,1280]{1,0:T(8,128)(2,1)}) %reduce-scatter.9.cloned.1.call-update) | async-done | bytes 2293776
  503.4 9.2 %reshape.110 = bf16[896,2,10,64]{3,2,1,0:T(8,128)(2,1)} reshape(bf16[896,1280]{1,0:T(8,128)(2,1)} %reduce-scatter.9.cloned.1.call-done) | data formatting | bytes 4587520
  512.6 7.9 %copy.35 = bf16[64,2,10,896]{3,0,2,1:T(8,128)(2,1)S(1)} copy(bf16[64,2,10,896]{0,2,1,3:T(8,128)(2,1)} %bitcast.69) | data formatting | bytes 4587520
  520.5 2.9 copy.27
  523.4 10.8 %all-to-all-start.1 = ((bf16[64,20,896]{2,1,0:T(8,128)(2,1)}), bf16[64,20,896]{2,1,0:T(8,128)(2,1)}, u32[]{:S(2)}, u32[]{:S(2)}) async-start(bf16[64,20,896]{2,1,0:T(8,128)(2,1)} %copy.27), calls=%async_computation.1 | async-start | bytes 5505024 | tf_op jit(solution)/shard_map/all_to_all | solution.py:66
  534.2 0.0 reduce-scatter.7.cloned.1.call-start
  534.2 0.0 all-gather.4.cloned.1.call-done
  534.2 1.9 fusion.45
  536.2 0.0 copy-start.1
  536.2 43.8 %all-gather.6.cloned.1.call-done = bf16[3584,256]{1,0:T(8,128)(2,1)} async-done(((bf16[56,256]{1,0:T(8,128)(2,1)}), bf16[3584,256]{1,0:T(8,128)(2,1)}) %all-gather.6.cloned.1.call-update) | async-done | bytes 1835024 | tf_op jit(solution)/shard_map/all_gather | solution.py:53
  580.0 76.6 %all-gather.8.cloned.1.call-done = bf16[256,3584]{0,1:T(8,128)(2,1)} async-done(((bf16[256,56]{0,1:T(8,128)(2,1)}), bf16[256,3584]{0,1:T(8,128)(2,1)}) %all-gather.8.cloned.1.call-update) | async-done | bytes 1835024 | tf_op jit(solution)/shard_map/all_gather | solution.py:58
  656.6 3.4 convolution_convert_fusion
  660.0 1.3 copy.32
  661.3 0.0 reduce-scatter.7.cloned.1.call-update
  661.3 0.0 copy-done.1
  661.3 0.1 copy.28
  661.4 21.1 %reduce-scatter.7.cloned.1.call-done = bf16[896,128]{1,0:T(8,128)(2,1)} async-done(((bf16[3584,128]{1,0:T(8,128)(2,1)}), bf16[896,128]{1,0:T(8,128)(2,1)}) %reduce-scatter.7.cloned.1.call-update) | async-done | bytes 229392
  682.6 1.1 copy.33
  683.6 0.0 all-to-all-done.1
  683.7 5.0 reshape.78
  688.6 8.4 %gather_fusion.1 = f32[1024,896]{1,0:T(8,128)} fusion(f32[1280,896]{1,0:T(8,128)} %reshape.78, s32[1024]{0:T(1024)S(1)} %broadcast_clamp_fusion), kind=kCustom, calls=%fused_computation.1 | custom fusion | bytes 7344128 | tf_op jit(solution)/shard_map/gather | solution.py:70
  697.0 3.1 fusion.5
  700.1 0.7 add_convert_fusion
  (10 shorter events, 0.1 us)
Async XLA Ops:
  7.4 7.3 %copy-start = (bf16[128,896]{1,0:T(8,128)(2,1)S(1)}, bf16[128,896]{1,0:T(8,128)(2,1)}, u32[]{:S(2)}) copy-start(bf16[128,896]{1,0:T(8,128)(2,1)} %param.9) | copy-start | bytes 688132
  7.4 496.1 %reduce-scatter.9.cloned.1.call-start = ((), (), s32[]{:S(2)}) async-start(), calls=%async_computation.8 | async-start | bytes 11468800
  417.4 116.9 %all-gather.4.cloned.1.call-start = ((), (), s32[]{:S(2)}) async-start(), calls=%async_computation.4 | async-start | bytes 1863680 | tf_op jit(solution)/shard_map/all_gather | solution.py:50
  417.9 162.1 %all-gather.6.cloned.1.call-start = ((), (), s32[]{:S(2)}) async-start(), calls=%async_computation.5 | async-start | bytes 1863680 | tf_op jit(solution)/shard_map/all_gather | solution.py:53
  418.5 238.0 %all-gather.8.cloned.1.call-start = ((), (), s32[]{:S(2)}) async-start(), calls=%async_computation.6 | async-start | bytes 1863680 | tf_op jit(solution)/shard_map/all_gather | solution.py:58
  523.4 160.2 %all-to-all-start.1 = ((bf16[64,20,896]{2,1,0:T(8,128)(2,1)}), bf16[64,20,896]{2,1,0:T(8,128)(2,1)}, u32[]{:S(2)}, u32[]{:S(2)}) async-start(bf16[64,20,896]{2,1,0:T(8,128)(2,1)} %copy.27), calls=%async_computation.1 | async-start | bytes 5505024 | tf_op jit(solution)/shard_map/all_to_all | solution.py:66
  534.2 148.4 %reduce-scatter.7.cloned.1.call-start = ((), (), s32[]{:S(2)}) async-start(), calls=%async_computation.7 | async-start | bytes 1146880
  536.2 125.1 %copy-start.1 = (f32[128,8]{0,1:T(8,128)S(1)}, f32[128,8]{0,1:T(8,128)}, u32[]{:S(2)}) copy-start(f32[128,8]{0,1:T(8,128)} %param.11) | copy-start | bytes 12292
Sparse Core Ops, SparseCore 0:
  417.5 85.9 reduce-scatter.8
  661.4 21.0 reduce-scatter.6
Sparse Core Ops, SparseCore 1:
  420.5 74.0 all-gather.3
  497.1 82.8 all-gather.5
  582.5 74.0 all-gather.7
where the time goes:
time: 711 us; the launch traced here: 708 us
  blocking collectives  270 us (38%)
  waiting for transfers between devices  227 us (32%)
  local copies, waits for them, and re-layouts  147 us (21%)
  matrix products  26.9 us (4%)
  between operations  15.2 us (2%)
  starting transfers between devices  11.1 us (2%)
  other arithmetic  11 us (2%)
    all_to_all x1, blocking collectives, body(): lax.all_to_all(outgoing.reshape(exp_count, local_experts * capacity, widt...  256 us
    unnamed x7, waiting for transfers between devices  107 us
    unnamed x12, local copies, waits for them, and re-layouts  94.2 us
    all_gather x1, waiting for transfers between devices, body(): lax.all_gather(s_down, 'exp', axis=1, tiled=True)  76.6 us
    all_gather x1, waiting for transfers between devices, body(): lax.all_gather(s_up, 'exp', axis=0, tiled=True)  43.8 us
    gather x2, local copies, waits for them, and re-layouts, body(): outgoing = jnp.where(keep, whole[token_of], zero_value)  21 us
    dot_general x1, matrix products, body(): jnp.einsum('sech,ehd->secd', hidden, w_down, preferred_element_type=jnp.f...  14.4 us
  transfers between devices with their start and end apart: 6, of which 4 were waited for; matrix products, arithmetic and copies ran while one was open for 4% of the time, Pallas kernels for 0%

commit v1 on v0

v1 whole, which is shorter than its diff:
```python
import functools

import jax
import jax.numpy as jnp
from jax import lax
from jax.experimental import pallas as pl
from jax.experimental.pallas import tpu as pltpu
from jax.sharding import PartitionSpec as P

MESH = pl.DeviceIdType.MESH
NY = 4
NC = 2
LANES = 128


def dims_of(exp_count):
    nz, nx = {64: (8, 4), 4: (2, 1)}[exp_count]
    return nz, nx


def routed_kernel(
    nz, nd, cap, tok, top, chunks, hid,
    tokens_ref, ids_ref, wts_ref, wg_hbm, wu_hbm, wd_hbm,
    out_ref,
    wg, wu, wd, meta_src, meta, sel, cmb_rows, cmb, held, packed, rows, gate, upper, hidden,
    outs, back, part, home,
    load_sem, wd_send, wd_recv, meta_send, meta_recv, z_send, z_recv, x_send, x_recv,
    y_send, y_recv, b_send, b_recv, h_send, h_recv,
):
    quarter = chunks * LANES
    grp = nz * cap
    f32, bf16 = jnp.float32, jnp.bfloat16
    exp = lax.axis_index("exp")
    y = lax.axis_index("tp")
    z = exp // nd
    d = exp % nd
    right = (y + 1) % NY
    left = (y + NY - 1) % NY
    across = (y + 2) % NY

    def z_peer(j):
        return (((z + j) % nz) * nd + d, y)

    def d_peer(r):
        return (z * nd + (d + r) % nd, y)

    def y_peer(q):
        return (exp, q)

    def send(src, dst, ss, rs, dev):
        pltpu.make_async_remote_copy(
            src_ref=src, dst_ref=dst, send_sem=ss, recv_sem=rs, device_id=dev, device_id_type=MESH
        ).start()

    def wait(ref, sem):
        pltpu.make_async_copy(ref, ref, sem).wait()

    load_g = pltpu.make_async_copy(wg_hbm, wg, load_sem.at[0])
    load_u = pltpu.make_async_copy(wu_hbm, wu, load_sem.at[1])
    load_d = pltpu.make_async_copy(wd_hbm.at[:, :, pl.ds(y * quarter, quarter)], wd.at[0], load_sem.at[2])
    load_g.start()
    load_u.start()
    load_d.start()

    barrier = pltpu.get_barrier_semaphore()
    for j in range(1, nz):
        pl.semaphore_signal(barrier, inc=1, device_id=z_peer(j), device_id_type=MESH)
    for r in range(1, nd):
        pl.semaphore_signal(barrier, inc=1, device_id=d_peer(r), device_id_type=MESH)
    for q in (left, right, across):
        pl.semaphore_signal(barrier, inc=1, device_id=y_peer(q), device_id_type=MESH)

    experts = nz * nd * 2
    lane = lax.broadcasted_iota(jnp.int32, (tok, experts), 1)
    named = jnp.zeros((tok, experts), f32)
    weight = jnp.zeros((tok, experts), f32)
    for k in range(top):
        hit = ids_ref[:, k:k + 1] == lane
        named = named + jnp.where(hit, 1.0, 0.0)
        weight = weight + jnp.where(hit, wts_ref[:, k:k + 1], 0.0)
    named_t = named.T
    before = lax.broadcasted_iota(jnp.int32, (tok, tok), 0) < lax.broadcasted_iota(jnp.int32, (tok, tok), 1)
    rank = jnp.dot(
        named_t.astype(bf16), jnp.where(before, 1.0, 0.0).astype(bf16), preferred_element_type=f32
    )
    meta_src[0] = jnp.where(named_t > 0.5, rank, -1.0)
    meta_src[1] = weight.T
    plane = 2 * nd

    pl.semaphore_wait(barrier, nz - 1 + nd - 1 + 3)

    for j in range(1, nz):
        zj = (z + j) % nz
        send(
            meta_src.at[:, pl.ds(pl.multiple_of(zj * plane, plane), plane), :],
            meta.at[:, :, pl.ds(j * tok, tok)],
            meta_send, meta_recv, z_peer(j),
        )
    meta[:, :, 0:tok] = meta_src[:, pl.ds(pl.multiple_of(z * plane, plane), plane), :]

    def send_tokens(k, carry):
        cols = pl.ds(pl.multiple_of(k * LANES, LANES), LANES)
        for j in range(1, nz):
            send(tokens_ref.at[:, cols], held.at[k, j], z_send.at[k], z_recv.at[k], z_peer(j))
        held[k, 0] = tokens_ref[:, cols]
        return carry

    lax.fori_loop(0, chunks, send_tokens, 0)

    for slot, q in ((1, right), (2, left), (3, across)):
        send(
            wd_hbm.at[:, :, pl.ds(pl.multiple_of(q * quarter, LANES), quarter)],
            wd.at[slot], wd_send.at[slot - 1], wd_recv.at[slot - 1], y_peer(q),
        )

    wait(meta.at[:, :, pl.ds(tok, (nz - 1) * tok)], meta_recv)

    row = lax.broadcasted_iota(jnp.int32, (grp, nz * tok), 0)
    col = lax.broadcasted_iota(jnp.int32, (grp, nz * tok), 1)
    wanted = jnp.where(row % nz == col // tok, row // nz, -5).astype(f32)

    def build(g, carry):
        r = g // 2
        index = ((d + r) % nd) * 2 + g % 2
        hit = meta[0, pl.ds(index, 1), :] == wanted
        sel[g] = jnp.where(hit, 1.0, 0.0).astype(bf16)
        cmb_rows[pl.ds(pl.multiple_of(g * grp, 16), grp), :] = jnp.where(
            hit, meta[1, pl.ds(index, 1), :], 0.0
        ).astype(bf16)
        return carry

    lax.fori_loop(0, 2 * nd, build, 0)

    gate[...] = jnp.zeros_like(gate)
    upper[...] = jnp.zeros_like(upper)

    def select(k, r):
        picked = jnp.dot(
            sel[pl.ds(2 * r, 2)].reshape(2 * grp, nz * tok),
            held[k].reshape(nz * tok, LANES),
            preferred_element_type=f32,
        )
        return picked.astype(bf16).reshape(2, grp, LANES)

    def stage_a(k):
        wait(held.at[k, pl.ds(1, nz - 1)], z_recv.at[k])

        def one(r, carry):
            packed[k, r] = select(k, r)
            send(packed.at[k, r], rows.at[0, k, :, r], x_send.at[k], x_recv.at[k], d_peer(r))
            return carry

        lax.fori_loop(1, nd, one, 0)
        rows[0, k, :, 0] = select(k, 0)

    def stage_b(k):
        wait(rows.at[0, k, :, pl.ds(1, nd - 1)], x_recv.at[k])
        send(rows.at[0, k], rows.at[1, k], y_send.at[0, k], y_recv.at[0, k], y_peer(right))
        send(rows.at[0, k], rows.at[2, k], y_send.at[1, k], y_recv.at[1, k], y_peer(left))

    halves = nd // 2

    def accumulate(k, slots):
        def one(i, carry):
            e = i // 2
            h = i % 2
            g = gate[e, h]
            u = upper[e, h]
            for s, q in slots:
                x = rows[s, k, e, pl.ds(h * halves, halves)].reshape(halves * grp, LANES)
                at = pl.ds(pl.multiple_of(q * quarter + k * LANES, LANES), LANES)
                g = g + jnp.dot(x, wg[e, at, :], preferred_element_type=f32)
                u = u + jnp.dot(x, wu[e, at, :], preferred_element_type=f32)
            gate[e, h] = g
            upper[e, h] = u
            return carry

        lax.fori_loop(0, 4, one, 0)

    def stage_c(k):
        wait(rows.at[1, k], y_recv.at[0, k])
        send(rows.at[1, k, 0], rows.at[3, k, 0], y_send.at[2, k], y_recv.at[2, k], y_peer(right))
        wait(rows.at[2, k], y_recv.at[1, k])
        send(rows.at[2, k, 1], rows.at[3, k, 1], y_send.at[3, k], y_recv.at[3, k], y_peer(left))
        accumulate(k, ((0, y), (1, left), (2, right)))

    def stage_d(k):
        wait(rows.at[3, k, 0], y_recv.at[2, k])
        wait(rows.at[3, k, 1], y_recv.at[3, k])
        accumulate(k, ((3, across),))

    load_g.wait()
    load_u.wait()

    lag_b, lag_c, lag_d = 1, 2, 4

    def step(i, carry):
        @pl.when(i < chunks)
        def _():
            stage_a(i)

        @pl.when((i >= lag_b) & (i < chunks + lag_b))
        def _():
            stage_b(i - lag_b)

        @pl.when((i >= lag_c) & (i < chunks + lag_c))
        def _():
            stage_c(i - lag_c)

        @pl.when(i >= lag_d)
        def _():
            stage_d(i - lag_d)

        return carry

    lax.fori_loop(0, chunks + lag_d, step, 0)

    half_rows = halves * grp
    for e in range(2):
        for h in range(2):
            g = gate[e, h]
            hidden[0, e, h * half_rows:(h + 1) * half_rows, :] = (
                g / (1.0 + jnp.exp(-g)) * upper[e, h]
            ).astype(bf16)
        u = chunks + e
        send(hidden.at[0, e], hidden.at[1, e], y_send.at[0, u], y_recv.at[0, u], y_peer(right))
        send(hidden.at[0, e], hidden.at[2, e], y_send.at[1, u], y_recv.at[1, u], y_peer(left))

    def turn(a, carry):
        block = pl.ds(pl.multiple_of(a * LANES, LANES), LANES)
        cmb[:, block] = cmb_rows[block, :].astype(f32).T.astype(bf16)
        return carry

    lax.fori_loop(0, 2 * nd * grp // LANES, turn, 0)

    low, high = pl.ds(0, half_rows), pl.ds(half_rows, half_rows)
    for e in range(2):
        u = chunks + e
        wait(hidden.at[1, e], y_recv.at[0, u])
        send(hidden.at[1, e, low], hidden.at[3, e, low], y_send.at[2, u], y_recv.at[2, u], y_peer(right))
        wait(hidden.at[2, e], y_recv.at[1, u])
        send(hidden.at[2, e, high], hidden.at[3, e, high], y_send.at[3, u], y_recv.at[3, u], y_peer(left))
    load_d.wait()
    for slot in (1, 2, 3):
        wait(wd.at[slot], wd_recv.at[slot - 1])
    for e in range(2):
        u = chunks + e
        wait(hidden.at[3, e, low], y_recv.at[2, u])
        wait(hidden.at[3, e, high], y_recv.at[3, u])

    def stage_e(k):
        cols = pl.ds(pl.multiple_of(k * LANES, LANES), LANES)
        for e in range(2):
            total = jnp.zeros((nd * grp, LANES), f32)
            for s in range(NY):
                total = total + jnp.dot(hidden[s, e], wd[s, e, :, cols], preferred_element_type=f32)
            value = total.astype(bf16).reshape(nd, grp, LANES)
            outs[k, :, e] = value
            back[k, 0, e] = value[0]

        def one(r, carry):
            send(outs.at[k, r], back.at[k, r], b_send.at[k], b_recv.at[k], d_peer(nd - r))
            return carry

        lax.fori_loop(1, nd, one, 0)

    def stage_f(k):
        wait(back.at[k, pl.ds(1, nd - 1)], b_recv.at[k])
        per = nz // 2
        for i in range(2):
            value = jnp.dot(
                cmb[i * per * tok:(i + 1) * per * tok, :],
                back[k].reshape(2 * nd * grp, LANES),
                preferred_element_type=f32,
            ).astype(bf16).reshape(per, tok, LANES)
            part[k, i * per:(i + 1) * per] = value
            for j in range(max(1, i * per), (i + 1) * per):
                send(part.at[k, j], home.at[k, j], h_send.at[k], h_recv.at[k], z_peer(nz - j))

    def stage_g(k):
        wait(home.at[k, pl.ds(1, nz - 1)], h_recv.at[k])
        total = part[k, 0].astype(f32)
        for j in range(1, nz):
            total = total + home[k, j].astype(f32)
        out_ref[:, pl.ds(pl.multiple_of(k * LANES, LANES), LANES)] = total

    lag_f, lag_g = 1, 3

    def step_back(i, carry):
        @pl.when(i < chunks)
        def _():
            stage_e(i)

        @pl.when((i >= lag_f) & (i < chunks + lag_f))
        def _():
            stage_f(i - lag_f)

        @pl.when(i >= lag_g)
        def _():
            stage_g(i - lag_g)

        return carry

    lax.fori_loop(0, chunks + lag_g, step_back, 0)

    wait(meta.at[:, :, pl.ds(tok, (nz - 1) * tok)], meta_send)
    for slot in (1, 2, 3):
        wait(wd.at[slot], wd_send.at[slot - 1])

    def drain(k, carry):
        wait(held.at[k, pl.ds(1, nz - 1)], z_send.at[k])
        wait(packed.at[k, pl.ds(1, nd - 1)], x_send.at[k])
        wait(rows.at[0, k], y_send.at[0, k])
        wait(rows.at[0, k], y_send.at[1, k])
        wait(rows.at[1, k, 0], y_send.at[2, k])
        wait(rows.at[2, k, 1], y_send.at[3, k])
        wait(outs.at[k, pl.ds(1, nd - 1)], b_send.at[k])
        wait(part.at[k, pl.ds(1, nz - 1)], h_send.at[k])
        return carry

    lax.fori_loop(0, chunks, drain, 0)
    for e in range(2):
        u = chunks + e
        wait(hidden.at[0, e], y_send.at[0, u])
        wait(hidden.at[0, e], y_send.at[1, u])
        wait(hidden.at[1, e, low], y_send.at[2, u])
        wait(hidden.at[2, e, high], y_send.at[3, u])


def routed(tokens, expert_ids, gate_weights, w_gate, w_up, w_down, cap):
    nz, nx = dims_of(lax.axis_size("exp"))
    nd = nx * NC
    tok, quarter = tokens.shape
    top = expert_ids.shape[1]
    width, hid = w_gate.shape[1:]
    chunks = quarter // LANES
    grp = nz * cap
    f32, bf16 = jnp.float32, jnp.bfloat16
    dma = pltpu.SemaphoreType.DMA
    vm = pltpu.VMEM
    slots = 2 * nd * grp
    hbm = pl.BlockSpec(memory_space=pl.ANY)
    inside = pl.BlockSpec(memory_space=pltpu.VMEM)
    return pl.pallas_call(
        functools.partial(routed_kernel, nz, nd, cap, tok, top, chunks, hid),
        out_shape=jax.ShapeDtypeStruct((tok, quarter), f32),
        in_specs=[inside, inside, inside, hbm, hbm, hbm],
        out_specs=inside,
        scratch_shapes=[
            vm((2, width, hid), bf16),
            vm((2, width, hid), bf16),
            vm((NY, 2, hid, quarter), bf16),
            vm((2, 2 * nz * nd, tok), f32),
            vm((2, 2 * nd, nz * tok), f32),
            vm((2 * nd, grp, nz * tok), bf16),
            vm((slots, nz * tok), bf16),
            vm((nz * tok, slots), bf16),
            vm((chunks, nz, tok, LANES), bf16),
            vm((chunks, nd, 2, grp, LANES), bf16),
            vm((NY, chunks, 2, nd, grp, LANES), bf16),
            vm((2, 2, nd // 2 * grp, hid), f32),
            vm((2, 2, nd // 2 * grp, hid), f32),
            vm((NY, 2, nd * grp, hid), bf16),
            vm((chunks, nd, 2, grp, LANES), bf16),
            vm((chunks, nd, 2, grp, LANES), bf16),
            vm((chunks, nz, tok, LANES), bf16),
            vm((chunks, nz, tok, LANES), bf16),
            dma((3,)), dma((3,)), dma((3,)), dma, dma,
            dma((chunks,)), dma((chunks,)), dma((chunks,)), dma((chunks,)),
            dma((4, chunks + 2)), dma((4, chunks + 2)),
            dma((chunks,)), dma((chunks,)), dma((chunks,)), dma((chunks,)),
        ],
        compiler_params=pltpu.CompilerParams(
            collective_id=0, has_side_effects=True, vmem_limit_bytes=60 * 1024 * 1024
        ),
        cost_estimate=pl.CostEstimate(
            flops=2 * slots * width * hid * 3, bytes_accessed=6 * width * hid * 2, transcendentals=slots * hid
        ),
        name="routed",
    )(tokens, expert_ids, gate_weights, w_gate, w_up, w_down)


def body(tokens, expert_ids, gate_weights, w_gate, w_up, w_down, s_gate, s_up, s_down):
    exp_count = lax.axis_size("exp")
    tok_count, top_count = expert_ids.shape
    experts = w_gate.shape[0] * exp_count
    capacity = max(2, 5 * tok_count * top_count // (4 * experts))
    units = s_gate.shape[1]
    whole = lax.all_gather(tokens, "tp", axis=1, tiled=True)
    shard = jnp.concatenate([s_gate, s_up, s_down.T], axis=1)
    shared_w = lax.all_gather(shard, "exp", axis=0, tiled=True)
    routed_sum = routed(tokens, expert_ids, gate_weights, w_gate, w_up, w_down, capacity)
    both = jnp.dot(whole, shared_w[:, :2 * units], preferred_element_type=jnp.float32)
    shared_hidden = (jax.nn.silu(both[:, :units]) * both[:, units:]).astype(jnp.bfloat16)
    shared_part = lax.dot_general(
        shared_hidden, shared_w[:, 2 * units:], (((1,), (1,)), ((), ())), preferred_element_type=jnp.float32
    )
    shared_sum = lax.psum_scatter(
        shared_part.astype(jnp.bfloat16), "tp", scatter_dimension=1, tiled=True
    ).astype(jnp.float32)
    return (shared_sum + routed_sum).astype(jnp.bfloat16)


def solution(mesh):
    return jax.shard_map(
        body,
        mesh=mesh,
        in_specs=(
            P("exp", "tp"),
            P("exp", None),
            P("exp", None),
            P("exp", None, "tp"),
            P("exp", None, "tp"),
            P("exp", "tp", None),
            P("exp", "tp"),
            P("exp", "tp"),
            P("tp", "exp"),
        ),
        out_specs=P("exp", "tp"),
        check_vma=False,
    )
```

time: 711 us -> 317 us (0.45)
  blocking collectives: 270 us -> 14.1 us
  Pallas kernels: 0 us -> 205 us
  waiting for transfers between devices: 227 us -> 72.4 us
  local copies, waits for them, and re-layouts: 147 us -> 3.82 us
  matrix products: 26.9 us -> 5.45 us
  starting transfers between devices: 11.1 us -> 0.04 us
  other arithmetic: 11 us -> 3.17 us
    all_to_all x1 -> x0, blocking collectives: 256 us -> none  [body(): lax.all_to_all(outgoing.reshape(exp_count, local_experts * capacity, widt...]
    pallas_call x0 -> x1, Pallas kernels: none -> 205 us  [routed(): pl.pallas_call(functools.partial(routed_kernel, nz, nd, cap, tok, top, ch...]
    unnamed x7 -> x3, waiting for transfers between devices: 107 us -> 0.05 us
    unnamed x12 -> x8, local copies, waits for them, and re-layouts: 94.2 us -> 3.82 us
    all_gather x3 -> x1, waiting for transfers between devices: 120 us -> 72.4 us  [body(): shared_w = lax.all_gather(shard, 'exp', axis=0, tiled=True)]
    gather x3 -> x0, local copies, waits for them, and re-layouts: 29.4 us -> none  [the longest x2 21 us: body(): outgoing = jnp.where(keep, whole[token_of], zero_value)]
    dot_general x4 -> x2, matrix products: 26.9 us -> 5.45 us  [the longest x1 3.18 us: body(): jnp.dot(whole, shared_w[:, :2 * units], preferred_element_type=jnp.float32)]
    all_to_all x1 -> x0, starting transfers between devices: 10.8 us -> none  [body(): lax.all_to_all(results.astype(jnp.bfloat16), 'exp', split_axis=0, concat_...]
  transfers between devices with their start and end apart: 6 -> 2, of which waited for: 4 -> 1; matrix products, arithmetic and copies ran while one was open for 4% -> 0% of each run, Pallas kernels for 0% -> 65%
where the time goes in v1:
time: 317 us
  Pallas kernels  205 us (65%)
  waiting for transfers between devices  72.4 us (23%)
  blocking collectives  14.1 us (4%)
  between operations  13.5 us (4%)
  matrix products  5.45 us (2%)
  local copies, waits for them, and re-layouts  3.82 us (1%)
  other arithmetic  3.17 us (1%)
    pallas_call x1, Pallas kernels, routed(): pl.pallas_call(functools.partial(routed_kernel, nz, nd, cap, tok, top, ch...  205 us
    all_gather x1, waiting for transfers between devices, body(): shared_w = lax.all_gather(shard, 'exp', axis=0, tiled=True)  72.4 us
    all_gather x1, blocking collectives, body(): whole = lax.all_gather(tokens, 'tp', axis=1, tiled=True)  14.1 us
  transfers between devices with their start and end apart: 2, of which 1 were waited for; matrix products, arithmetic and copies ran while one was open for 0% of the time, Pallas kernels for 65%

profile of v1, /device:TPU:1, one launch (start us, length us, event | category | flops | bytes accessed | tf_op | source)
XLA Modules:
  0.0 317.1 jit_solution(16139632499294598513)
XLA Ops:
  6.5 0.0 all-gather.2.cloned.1.call-start
  6.5 1.4 pad_maximum_fusion
  8.0 0.0 all-gather.2.cloned.1.call-update
  8.0 0.0 reduce-scatter.4.cloned.1.call-start
  8.0 14.1 %all_gather.7 = bf16[128,3584]{1,0:T(8,128)(2,1)S(1)} all-gather(bf16[128,896]{1,0:T(8,128)(2,1)} %tokens_ref.1), channel_id=1, replica_groups=mesh['exp'=64,'tp'=4] {'tp'}, dimensions={1}, use_global_device_ids=true | all-gather | bytes 1146880 | tf_op jit(solution)/shard_map/all_gather | solution.py:389
  22.1 72.4 %all-gather.2.cloned.1.call-done = bf16[3584,768]{1,0:T(8,128)(2,1)} async-done(((bf16[56,768]{1,0:T(8,128)(2,1)}), bf16[3584,768]{1,0:T(8,128)(2,1)}) %all-gather.2.cloned.1.call-update) | async-done | bytes 5505040 | tf_op jit(solution)/shard_map/all_gather | solution.py:391
  94.5 3.2 %fusion.3 = f32[128,512]{0,1:T(8,128)S(1)} fusion(bf16[128,3584]{1,0:T(8,128)(2,1)S(1)} %all_gather.7, bf16[3584,768]{1,0:T(8,128)(2,1)} %all-gather.2.cloned.1.call-done), kind=kOutput, calls=%fused_computation.4 | convolution fusion | flops 469762048 | bytes 4849664 | tf_op jit(solution)/shard_map/dot_general | solution.py:393
  97.7 0.0 copy-start
  97.7 0.0 copy-start.1
  97.7 2.3 convolution_convert_fusion
  100.0 1.3 copy.14
  101.3 0.0 reduce-scatter.4.cloned.1.call-update
  101.3 0.0 copy-done
  101.3 0.7 copy.12.ids_ref
  102.0 0.0 copy-done.1
  102.0 0.7 copy.13.wts_ref
  102.7 204.6 %routed.1 = f32[128,896]{1,0:T(8,128)} custom-call(bf16[128,896]{1,0:T(8,128)(2,1)} %tokens_ref.1, s32[128,8]{1,0:T(8,128)} %copy.12.ids_ref, f32[128,8]{1,0:T(8,128)} %copy.13.wts_ref, bf16[2,3584,256]{2,1,0:T(8,128)(2,1)} %wg_hbm.1, bf16[2,3584,256]{2,1,0:T(8,128)(2,1)} %wu_hbm.1, bf16[2,256,3584]{2,1,0:T(8,128)(2,1)} %wd_hbm.1), custom_call_target="tpu_custom_call" | custom-call | flops 7046430720 | bytes 11010048 | tf_op jit(solution)/shard_map/routed/pallas_call | solution.py:344
  307.4 0.0 reduce-scatter.4.cloned.1.call-done
  307.4 1.1 copy.15
  308.5 1.7 add_convert_fusion
Async XLA Ops:
  6.5 88.0 %all-gather.2.cloned.1.call-start = ((), (), s32[]{:S(2)}) async-start(), calls=%async_computation.1 | async-start | bytes 5591040 | tf_op jit(solution)/shard_map/all_gather | solution.py:391
  8.0 299.4 %reduce-scatter.4.cloned.1.call-start = ((), (), s32[]{:S(2)}) async-start(), calls=%async_computation.2 | async-start | bytes 1146880
  97.7 3.6 %copy-start = (s32[128,8]{0,1:T(8,128)S(1)}, s32[128,8]{0,1:T(8,128)}, u32[]{:S(2)}) copy-start(s32[128,8]{0,1:T(8,128)} %param.10) | copy-start | bytes 12292
  97.7 4.3 %copy-start.1 = (f32[128,8]{0,1:T(8,128)S(1)}, f32[128,8]{0,1:T(8,128)}, u32[]{:S(2)}) copy-start(f32[128,8]{0,1:T(8,128)} %param.11) | copy-start | bytes 12292
Sparse Core Ops, SparseCore 0:
  10.0 84.4 all-gather.1
  101.4 27.0 reduce-scatter.3

commit v2 on v1

--- a/solution.py
+++ b/solution.py
@@ -18,14 +18,16 @@
     return nz, nx
 
 
-def routed_kernel(
+def layer_kernel(
     nz, nd, cap, tok, top, chunks, hid,
-    tokens_ref, ids_ref, wts_ref, wg_hbm, wu_hbm, wd_hbm,
+    tokens_ref, ids_ref, wts_ref, wg_hbm, wu_hbm, wd_hbm, shard_ref,
     out_ref,
     wg, wu, wd, meta_src, meta, sel, cmb_rows, cmb, held, packed, rows, gate, upper, hidden,
     outs, back, part, home,
+    spread, shards, tokens_y, padded, pieces, pieces_y,
     load_sem, wd_send, wd_recv, meta_send, meta_recv, z_send, z_recv, x_send, x_recv,
     y_send, y_recv, b_send, b_recv, h_send, h_recv,
+    sz_send, sz_recv, sx_send, sx_recv, sc_send, sc_recv, t_send, t_recv, p_send, p_recv,
 ):
     quarter = chunks * LANES
     grp = nz * cap
@@ -46,6 +48,13 @@
 
     def y_peer(q):
         return (exp, q)
+
+    nx = nd // NC
+    x = d // NC
+    core = d % NC
+
+    def d_of(r, c):
+        return ((x + nx - r) % nx) * NC + c
 
     def send(src, dst, ss, rs, dev):
         pltpu.make_async_remote_copy(
@@ -98,6 +107,10 @@
         )
     meta[:, :, 0:tok] = meta_src[:, pl.ds(pl.multiple_of(z * plane, plane), plane), :]
 
+    y_slots = ((1, right), (2, left), (3, across))
+    for slot, q in y_slots:
+        send(tokens_ref, tokens_y.at[slot - 1], t_send.at[slot - 1], t_recv.at[slot - 1], y_peer(q))
+
     def send_tokens(k, carry):
         cols = pl.ds(pl.multiple_of(k * LANES, LANES), LANES)
         for j in range(1, nz):
@@ -107,7 +120,11 @@
 
     lax.fori_loop(0, chunks, send_tokens, 0)
 
-    for slot, q in ((1, right), (2, left), (3, across)):
+    for j in range(1, nz):
+        send(shard_ref, shards.at[:, j, d], sz_send, sz_recv, z_peer(j))
+    shards[:, 0, d] = shard_ref[...]
+
+    for slot, q in y_slots:
         send(
             wd_hbm.at[:, :, pl.ds(pl.multiple_of(q * quarter, LANES), quarter)],
             wd.at[slot], wd_send.at[slot - 1], wd_recv.at[slot - 1], y_peer(q),
@@ -189,6 +206,62 @@
         wait(rows.at[3, k, 1], y_recv.at[3, k])
         accumulate(k, ((3, across),))
 
+    def shards_in_plane():
+        wait(shards.at[:, pl.ds(1, nz - 1), d], sz_recv)
+        mine = shards.at[:, :, d]
+        for r in range(1, nx):
+            send(mine, mine, sx_send.at[r - 1], sx_recv.at[r - 1], (z * nd + ((x + r) % nx) * NC + core, y))
+        send(mine, mine, sc_send.at[0], sc_recv.at[0], (z * nd + x * NC + 1 - core, y))
+
+    def shards_in_chip():
+        for r in range(1, nx):
+            block = shards.at[:, :, d_of(r, core)]
+            wait(block, sx_recv.at[r - 1])
+            send(block, block, sc_send.at[r], sc_recv.at[r], (z * nd + x * NC + 1 - core, y))
+
+    rp = shard_ref.shape[1]
+    rs = quarter * NY // (nz * nd)
+    per_quarter = quarter // rs
+    run = min(per_quarter, nd)
+
+    def spread_matrix():
+        into = lax.broadcasted_iota(jnp.int32, spread.shape, 1)
+        at = lax.broadcasted_iota(jnp.int32, spread.shape, 0)
+        inner = into % rp
+        spread[...] = jnp.where((inner < rs) & (at == into // rp * rs + inner), 1.0, 0.0).astype(bf16)
+
+    def block_of(m, q, i):
+        first = q * per_quarter + i * run
+        zr = (z + nz - first // nd) % nz
+        return shards[m, zr, pl.ds(first % nd, run)].reshape(run * rp, hid)
+
+    def shared_expert():
+        for r in range(nx):
+            wait(shards.at[:, :, d_of(r, 1 - core)], sc_recv.at[r])
+        s_gate = jnp.zeros((tok, hid), f32)
+        s_upper = jnp.zeros((tok, hid), f32)
+        for slot, q in ((0, y), (1, left), (2, right), (3, across)):
+            if slot:
+                wait(tokens_y.at[slot - 1], t_recv.at[slot - 1])
+            source = tokens_y[slot - 1] if slot else tokens_ref[...]
+            padded[...] = jnp.dot(source, spread[...], preferred_element_type=f32).astype(bf16)
+            for i in range(per_quarter // run):
+                lhs = padded[:, i * run * rp:(i + 1) * run * rp]
+                s_gate = s_gate + jnp.dot(lhs, block_of(0, q, i), preferred_element_type=f32)
+                s_upper = s_upper + jnp.dot(lhs, block_of(1, q, i), preferred_element_type=f32)
+        act = (s_gate / (1.0 + jnp.exp(-s_gate)) * s_upper).astype(bf16)
+        across_rows = (((1,), (1,)), ((), ()))
+        for slot, q in ((1, right), (2, left), (3, across), (0, y)):
+            for i in range(per_quarter // run):
+                padded[:, i * run * rp:(i + 1) * run * rp] = lax.dot_general(
+                    act, block_of(2, q, i), across_rows, preferred_element_type=f32
+                ).astype(bf16)
+            pieces[slot] = lax.dot_general(
+                padded[...], spread[...], across_rows, preferred_element_type=f32
+            ).astype(bf16)
+            if slot:
+                send(pieces.at[slot], pieces_y.at[slot - 1], p_send.at[slot - 1], p_recv.at[slot - 1], y_peer(q))
+
     load_g.wait()
     load_u.wait()
 
@@ -198,6 +271,15 @@
         @pl.when(i < chunks)
         def _():
             stage_a(i)
+
+        @pl.when(i == 3)
+        def _():
+            shards_in_plane()
+
+        @pl.when(i == chunks)
+        def _():
+            spread_matrix()
+            shards_in_chip()
 
         @pl.when((i >= lag_b) & (i < chunks + lag_b))
         def _():
@@ -225,6 +307,8 @@
         u = chunks + e
         send(hidden.at[0, e], hidden.at[1, e], y_send.at[0, u], y_recv.at[0, u], y_peer(right))
         send(hidden.at[0, e], hidden.at[2, e], y_send.at[1, u], y_recv.at[1, u], y_peer(left))
+
+    shared_expert()
 
     def turn(a, carry):
         block = pl.ds(pl.multiple_of(a * LANES, LANES), LANES)
@@ -278,11 +362,19 @@
                 send(part.at[k, j], home.at[k, j], h_send.at[k], h_recv.at[k], z_peer(nz - j))
 
     def stage_g(k):
+        @pl.when(k == 0)
+        def _():
+            for slot in (1, 2, 3):
+                wait(pieces_y.at[slot - 1], p_recv.at[slot - 1])
+
+        cols = pl.ds(pl.multiple_of(k * LANES, LANES), LANES)
         wait(home.at[k, pl.ds(1, nz - 1)], h_recv.at[k])
-        total = part[k, 0].astype(f32)
+        total = part[k, 0].astype(f32) + pieces[0, :, cols].astype(f32)
+        for slot in (1, 2, 3):
+            total = total + pieces_y[slot - 1, :, cols].astype(f32)
         for j in range(1, nz):
             total = total + home[k, j].astype(f32)
-        out_ref[:, pl.ds(pl.multiple_of(k * LANES, LANES), LANES)] = total
+        out_ref[:, cols] = total.astype(bf16)
 
     lag_f, lag_g = 1, 3
 
@@ -304,7 +396,14 @@
     lax.fori_loop(0, chunks + lag_g, step_back, 0)
 
     wait(meta.at[:, :, pl.ds(tok, (nz - 1) * tok)], meta_send)
+    wait(shards.at[:, pl.ds(1, nz - 1), d], sz_send)
+    for r in range(nx):
+        if r:
+            wait(shards.at[:, :, d], sx_send.at[r - 1])
+        wait(shards.at[:, :, d_of(r, core)], sc_send.at[r])
     for slot in (1, 2, 3):
+        wait(tokens_y.at[slot - 1], t_send.at[slot - 1])
+        wait(pieces.at[slot], p_send.at[slot - 1])
         wait(wd.at[slot], wd_send.at[slot - 1])
 
     def drain(k, carry):
@@ -327,7 +426,7 @@
         wait(hidden.at[2, e, high], y_send.at[3, u])
 
 
-def routed(tokens, expert_ids, gate_weights, w_gate, w_up, w_down, cap):
+def layer(tokens, expert_ids, gate_weights, w_gate, w_up, w_down, shard, cap):
     nz, nx = dims_of(lax.axis_size("exp"))
     nd = nx * NC
     tok, quarter = tokens.shape
@@ -339,12 +438,14 @@
     dma = pltpu.SemaphoreType.DMA
     vm = pltpu.VMEM
     slots = 2 * nd * grp
+    rp = shard.shape[1]
+    padded_cols = quarter // (width // (nz * nd)) * rp
     hbm = pl.BlockSpec(memory_space=pl.ANY)
     inside = pl.BlockSpec(memory_space=pltpu.VMEM)
     return pl.pallas_call(
-        functools.partial(routed_kernel, nz, nd, cap, tok, top, chunks, hid),
-        out_shape=jax.ShapeDtypeStruct((tok, quarter), f32),
-        in_specs=[inside, inside, inside, hbm, hbm, hbm],
+        functools.partial(layer_kernel, nz, nd, cap, tok, top, chunks, hid),
+        out_shape=jax.ShapeDtypeStruct((tok, quarter), bf16),
+        in_specs=[inside, inside, inside, hbm, hbm, hbm, inside],
         out_specs=inside,
         scratch_shapes=[
             vm((2, width, hid), bf16),
@@ -365,10 +466,18 @@
             vm((chunks, nd, 2, grp, LANES), bf16),
             vm((chunks, nz, tok, LANES), bf16),
             vm((chunks, nz, tok, LANES), bf16),
+            vm((quarter, padded_cols), bf16),
+            vm((3, nz, nd, rp, hid), bf16),
+            vm((NY - 1, tok, quarter), bf16),
+            vm((tok, padded_cols), bf16),
+            vm((NY, tok, quarter), bf16),
+            vm((NY - 1, tok, quarter), bf16),
             dma((3,)), dma((3,)), dma((3,)), dma, dma,
             dma((chunks,)), dma((chunks,)), dma((chunks,)), dma((chunks,)),
             dma((4, chunks + 2)), dma((4, chunks + 2)),
             dma((chunks,)), dma((chunks,)), dma((chunks,)), dma((chunks,)),
+            dma, dma, dma((max(1, nx - 1),)), dma((max(1, nx - 1),)), dma((nx,)), dma((nx,)),
+            dma((3,)), dma((3,)), dma((3,)), dma((3,)),
         ],
         compiler_params=pltpu.CompilerParams(
             collective_id=0, has_side_effects=True, vmem_limit_bytes=60 * 1024 * 1024
@@ -376,8 +485,8 @@
         cost_estimate=pl.CostEstimate(
             flops=2 * slots * width * hid * 3, bytes_accessed=6 * width * hid * 2, transcendentals=slots * hid
         ),
-        name="routed",
-    )(tokens, expert_ids, gate_weights, w_gate, w_up, w_down)
+        name="layer",
+    )(tokens, expert_ids, gate_weights, w_gate, w_up, w_down, shard)
 
 
 def body(tokens, expert_ids, gate_weights, w_gate, w_up, w_down, s_gate, s_up, s_down):
@@ -385,20 +494,10 @@
     tok_count, top_count = expert_ids.shape
     experts = w_gate.shape[0] * exp_count
     capacity = max(2, 5 * tok_count * top_count // (4 * experts))
-    units = s_gate.shape[1]
-    whole = lax.all_gather(tokens, "tp", axis=1, tiled=True)
-    shard = jnp.concatenate([s_gate, s_up, s_down.T], axis=1)
-    shared_w = lax.all_gather(shard, "exp", axis=0, tiled=True)
-    routed_sum = routed(tokens, expert_ids, gate_weights, w_gate, w_up, w_down, capacity)
-    both = jnp.dot(whole, shared_w[:, :2 * units], preferred_element_type=jnp.float32)
-    shared_hidden = (jax.nn.silu(both[:, :units]) * both[:, units:]).astype(jnp.bfloat16)
-    shared_part = lax.dot_general(
-        shared_hidden, shared_w[:, 2 * units:], (((1,), (1,)), ((), ())), preferred_element_type=jnp.float32
-    )
-    shared_sum = lax.psum_scatter(
-        shared_part.astype(jnp.bfloat16), "tp", scatter_dimension=1, tiled=True
-    ).astype(jnp.float32)
-    return (shared_sum + routed_sum).astype(jnp.bfloat16)
+    rows = s_gate.shape[0]
+    shard = jnp.stack([s_gate, s_up, s_down.T])
+    shard = jnp.pad(shard, ((0, 0), (0, -rows % 64), (0, 0)))
+    return layer(tokens, expert_ids, gate_weights, w_gate, w_up, w_down, shard, capacity)
 
 
 def solution(mesh):

time: 317 us -> 246 us (0.78)
  waiting for transfers between devices: 72.4 us -> 0 us
  Pallas kernels: 205 us -> 240 us
  blocking collectives: 14.1 us -> 0 us
  between operations: 13.5 us -> 0.01 us
  matrix products: 5.45 us -> 0 us
    all_gather x1 -> x0, waiting for transfers between devices: 72.4 us -> none  [body(): shared_w = lax.all_gather(shard, 'exp', axis=0, tiled=True)]
    pallas_call x1, Pallas kernels: 205 us -> 240 us  [layer(): pl.pallas_call(functools.partial(layer_kernel, nz, nd, cap, tok, top, chu...]
    all_gather x1 -> x0, blocking collectives: 14.1 us -> none  [body(): whole = lax.all_gather(tokens, 'tp', axis=1, tiled=True)]
    dot_general x2 -> x0, matrix products: 5.45 us -> none  [the longest x1 3.18 us: body(): jnp.dot(whole, shared_w[:, :2 * units], preferred_element_type=jnp.float32)]
  transfers between devices with their start and end apart: 2 -> 0, of which waited for: 1 -> 0; matrix products, arithmetic and copies ran while one was open for 0% -> 0% of each run, Pallas kernels for 65% -> 0%
where the time goes in v2:
time: 246 us
  Pallas kernels  240 us (98%)
  local copies, waits for them, and re-layouts  4.47 us (2%)
    pallas_call x1, Pallas kernels, layer(): pl.pallas_call(functools.partial(layer_kernel, nz, nd, cap, tok, top, chu...  240 us

profile of v2, /device:TPU:1, one launch (start us, length us, event | category | flops | bytes accessed | tf_op | source)
XLA Modules:
  0.0 245.5 jit_solution(15362282924747767601)
XLA Ops:
  0.0 1.4 copy.10.ids_ref
  1.4 1.4 copy.11.wts_ref
  2.8 1.4 fusion.4.shard_ref
  4.3 239.6 %layer.1 = bf16[128,896]{1,0:T(8,128)(2,1)} custom-call(bf16[128,896]{1,0:T(8,128)(2,1)} %tokens_ref.1, s32[128,8]{1,0:T(8,128)} %copy.10.ids_ref, f32[128,8]{1,0:T(8,128)} %copy.11.wts_ref, bf16[2,3584,256]{2,1,0:T(8,128)(2,1)} %wg_hbm.1, bf16[2,3584,256]{2,1,0:T(8,128)(2,1)} %wu_hbm.1, bf16[2,256,3584]{2,1,0:T(8,128)(2,1)} %wd_hbm.1, ...), custom_call_target="tpu_custom_call" | custom-call | flops 7046430720 | bytes 11010048 | tf_op jit(solution)/shard_map/layer/pallas_call | solution.py:445
  243.9 1.6 copy.13

commit v3 on v2

v3 whole, which is shorter than its diff:
```python
import functools

import jax
import jax.numpy as jnp
from jax import lax
from jax.experimental import pallas as pl
from jax.experimental.pallas import tpu as pltpu
from jax.sharding import PartitionSpec as P

MESH = pl.DeviceIdType.MESH
NY = 4
NC = 2
LANES = 128


def dims_of(exp_count):
    nz, nx = {64: (8, 4), 4: (2, 1)}[exp_count]
    return nz, nx


def layer_kernel(
    nz, nd, cap, tok, top, chunks, hid,
    tokens_ref, ids_ref, wts_ref, wg_hbm, wu_hbm, wd_hbm, shard_ref,
    out_ref,
    wg, wu, wd, score, meta, sel, cmb, order, held, packed, rows, gate, upper, hidden,
    outs, back, part, home, turned,
    spread, shards, tokens_y, padded, pieces, pieces_y,
    load_sem, wd_send, wd_recv, meta_send, meta_recv, z_send, z_recv, x_send, x_recv,
    y_send, y_recv, b_send, b_recv, h_send, h_recv,
    sz_send, sz_recv, sx_send, sx_recv, sc_send, sc_recv, t_send, t_recv, p_send, p_recv,
):
    quarter = chunks * LANES
    grp = nz * cap
    f32, bf16 = jnp.float32, jnp.bfloat16
    exp = lax.axis_index("exp")
    y = lax.axis_index("tp")
    z = exp // nd
    d = exp % nd
    right = (y + 1) % NY
    left = (y + NY - 1) % NY
    across = (y + 2) % NY

    def z_peer(j):
        return (((z + j) % nz) * nd + d, y)

    def d_peer(r):
        return (z * nd + (d + r) % nd, y)

    def y_peer(q):
        return (exp, q)

    nx = nd // NC
    x = d // NC
    core = d % NC

    def d_of(r, c):
        return ((x + nx - r) % nx) * NC + c

    def send(src, dst, ss, rs, dev):
        pltpu.make_async_remote_copy(
            src_ref=src, dst_ref=dst, send_sem=ss, recv_sem=rs, device_id=dev, device_id_type=MESH
        ).start()

    def wait(ref, sem):
        pltpu.make_async_copy(ref, ref, sem).wait()

    load_g = pltpu.make_async_copy(wg_hbm, wg, load_sem.at[0])
    load_u = pltpu.make_async_copy(wu_hbm, wu, load_sem.at[1])
    load_d = pltpu.make_async_copy(wd_hbm.at[:, :, pl.ds(y * quarter, quarter)], wd.at[0], load_sem.at[2])
    load_g.start()
    load_u.start()
    load_d.start()

    barrier = pltpu.get_barrier_semaphore()
    for j in range(1, nz):
        pl.semaphore_signal(barrier, inc=1, device_id=z_peer(j), device_id_type=MESH)
    for r in range(1, nd):
        pl.semaphore_signal(barrier, inc=1, device_id=d_peer(r), device_id_type=MESH)
    for q in (left, right, across):
        pl.semaphore_signal(barrier, inc=1, device_id=y_peer(q), device_id_type=MESH)

    experts = nz * nd * 2
    names = lax.broadcasted_iota(jnp.int32, (experts, tok), 0)
    named = jnp.zeros((experts, tok), f32)
    weight = jnp.zeros((experts, tok), f32)
    for k in range(top):
        hit = ids_ref[k:k + 1, :] == names
        named = named + jnp.where(hit, 1.0, 0.0)
        weight = weight + jnp.where(hit, wts_ref[k:k + 1, :], 0.0)
    before = lax.broadcasted_iota(jnp.int32, (tok, tok), 0) < lax.broadcasted_iota(jnp.int32, (tok, tok), 1)
    rank = jnp.dot(
        named.astype(bf16), jnp.where(before, 1.0, 0.0).astype(bf16), preferred_element_type=f32
    )
    score[0] = jnp.where(named > 0.5, rank, -1.0)
    score[1] = weight
    plane = 2 * nd

    pl.semaphore_wait(barrier, nz - 1 + nd - 1 + 3)

    for j in range(1, nz):
        zj = (z + j) % nz
        send(
            score.at[0, pl.ds(pl.multiple_of(zj * plane, plane), plane), :],
            meta.at[:, pl.ds(j * tok, tok)],
            meta_send, meta_recv, z_peer(j),
        )
    meta[:, 0:tok] = score[0, pl.ds(pl.multiple_of(z * plane, plane), plane), :]

    y_slots = ((1, right), (2, left), (3, across))
    for slot, q in y_slots:
        send(tokens_ref, tokens_y.at[slot - 1], t_send.at[slot - 1], t_recv.at[slot - 1], y_peer(q))

    def send_tokens(k, carry):
        cols = pl.ds(pl.multiple_of(k * LANES, LANES), LANES)
        for j in range(1, nz):
            send(tokens_ref.at[:, cols], held.at[k, j], z_send.at[k], z_recv.at[k], z_peer(j))
        held[k, 0] = tokens_ref[:, cols]
        return carry

    lax.fori_loop(0, chunks, send_tokens, 0)

    for j in range(1, nz):
        send(shard_ref, shards.at[:, j, d], sz_send, sz_recv, z_peer(j))
    shards[:, 0, d] = shard_ref[...]

    for slot, q in y_slots:
        send(
            wd_hbm.at[:, :, pl.ds(pl.multiple_of(q * quarter, LANES), quarter)],
            wd.at[slot], wd_send.at[slot - 1], wd_recv.at[slot - 1], y_peer(q),
        )

    wait(meta.at[:, pl.ds(tok, (nz - 1) * tok)], meta_recv)

    row = lax.broadcasted_iota(jnp.int32, (grp, nz * tok), 0)
    col = lax.broadcasted_iota(jnp.int32, (grp, nz * tok), 1)
    wanted = jnp.where(row % nz == col // tok, row // nz, -5).astype(f32)

    def build(g, carry):
        index = ((d + g % nd) % nd) * 2 + g // nd
        hit = meta[pl.ds(index, 1), :] == wanted
        sel[g // nd, g % nd] = jnp.where(hit, 1.0, 0.0).astype(bf16)
        return carry

    lax.fori_loop(0, 2 * nd, build, 0)

    gate[...] = jnp.zeros_like(gate)
    upper[...] = jnp.zeros_like(upper)
    slots = nd * grp

    def stage_a(u):
        e = u // chunks
        k = u % chunks

        @pl.when(e == 0)
        def _():
            wait(held.at[k, pl.ds(1, nz - 1)], z_recv.at[k])

        packed[u] = jnp.dot(
            sel[e].reshape(slots, nz * tok), held[k].reshape(nz * tok, LANES), preferred_element_type=f32
        ).astype(bf16).reshape(nd, grp, LANES)
        for r in range(1, nd):
            send(packed.at[u, r], rows.at[0, u, r], x_send.at[u], x_recv.at[u], d_peer(r))
        rows[0, u, 0] = packed[u, 0]

    def stage_b(u):
        wait(rows.at[0, u, pl.ds(1, nd - 1)], x_recv.at[u])
        send(rows.at[0, u], rows.at[1, u], y_send.at[0, u], y_recv.at[0, u], y_peer(right))
        send(rows.at[0, u], rows.at[2, u], y_send.at[1, u], y_recv.at[1, u], y_peer(left))

    halves = nd // 2
    first, second = pl.ds(0, halves), pl.ds(halves, halves)

    def accumulate(u, sources):
        e = u // chunks
        k = u % chunks

        def one(h, carry):
            g = gate[e, h]
            up = upper[e, h]
            for s, q in sources:
                x = rows[s, u, pl.ds(h * halves, halves)].reshape(halves * grp, LANES)
                at = pl.ds(pl.multiple_of(q * quarter + k * LANES, LANES), LANES)
                g = g + jnp.dot(x, wg[e, at, :], preferred_element_type=f32)
                up = up + jnp.dot(x, wu[e, at, :], preferred_element_type=f32)
            gate[e, h] = g
            upper[e, h] = up
            return carry

        lax.fori_loop(0, 2, one, 0)

    def stage_c(u):
        wait(rows.at[1, u], y_recv.at[0, u])
        send(rows.at[1, u, first], rows.at[3, u, first], y_send.at[2, u], y_recv.at[2, u], y_peer(right))
        wait(rows.at[2, u], y_recv.at[1, u])
        send(rows.at[2, u, second], rows.at[3, u, second], y_send.at[3, u], y_recv.at[3, u], y_peer(left))
        accumulate(u, ((0, y), (1, left), (2, right)))

    def stage_d(u):
        wait(rows.at[3, u, first], y_recv.at[2, u])
        wait(rows.at[3, u, second], y_recv.at[3, u])
        accumulate(u, ((3, across),))

    half_rows = halves * grp
    low, high = pl.ds(0, half_rows), pl.ds(half_rows, half_rows)
    units = 2 * chunks

    def hidden_out(e):
        for h in range(2):
            g = gate[e, h]
            hidden[0, e, h * half_rows:(h + 1) * half_rows, :] = (
                g / (1.0 + jnp.exp(-g)) * upper[e, h]
            ).astype(bf16)
        u = units + e
        send(hidden.at[0, e], hidden.at[1, e], y_send.at[0, u], y_recv.at[0, u], y_peer(right))
        send(hidden.at[0, e], hidden.at[2, e], y_send.at[1, u], y_recv.at[1, u], y_peer(left))

    def hidden_on(e):
        u = units + e
        wait(hidden.at[1, e], y_recv.at[0, u])
        send(hidden.at[1, e, low], hidden.at[3, e, low], y_send.at[2, u], y_recv.at[2, u], y_peer(right))
        wait(hidden.at[2, e], y_recv.at[1, u])
        send(hidden.at[2, e, high], hidden.at[3, e, high], y_send.at[3, u], y_recv.at[3, u], y_peer(left))

    def hidden_in(e):
        u = units + e
        wait(hidden.at[3, e, low], y_recv.at[2, u])
        wait(hidden.at[3, e, high], y_recv.at[3, u])

    def stage_e(e, k):
        cols = pl.ds(pl.multiple_of(k * LANES, LANES), LANES)
        total = jnp.zeros((slots, LANES), f32)
        for s in range(NY):
            total = total + jnp.dot(hidden[s, e], wd[s, e, :, cols], preferred_element_type=f32)
        value = total.astype(bf16).reshape(nd, grp, LANES)
        outs[e, k] = value
        back[e, k, 0] = value[0]
        for r in range(1, nd):
            send(outs.at[e, k, r], back.at[e, k, r], b_send.at[e, k], b_recv.at[e, k], d_peer(nd - r))

    def stage_f(e, k):
        wait(back.at[e, k, pl.ds(1, nd - 1)], b_recv.at[e, k])
        value = jnp.dot(
            order[...], back[e, k].reshape(slots, LANES), preferred_element_type=f32
        ).astype(bf16).reshape(nz, nd * cap, LANES)
        part[e, k] = value
        home[e, k, 0] = value[0]
        for j in range(1, nz):
            send(part.at[e, k, j], home.at[e, k, j], h_send.at[e, k], h_recv.at[e, k], z_peer(nz - j))

    def stage_g(k):
        @pl.when(k == 0)
        def _():
            for slot in (1, 2, 3):
                wait(pieces_y.at[slot - 1], p_recv.at[slot - 1])

        cols = pl.ds(pl.multiple_of(k * LANES, LANES), LANES)
        total = pieces[0, :, cols].astype(f32)
        for slot in (1, 2, 3):
            total = total + pieces_y[slot - 1, :, cols].astype(f32)
        for e in range(2):
            wait(home.at[e, k, pl.ds(1, nz - 1)], h_recv.at[e, k])
            total = total + jnp.dot(
                cmb[e], home[e, k].reshape(nz * nd * cap, LANES), preferred_element_type=f32
            )
        out_ref[:, cols] = total.astype(bf16)

    def build_return():
        at = lax.broadcasted_iota(jnp.int32, (slots, slots), 0)
        lane = lax.broadcasted_iota(jnp.int32, (1, slots), 1)
        source = lane % grp
        target = (source % nz) * (nd * cap) + source // nz * nd + (d + lane // grp) % nd
        order[...] = jnp.where(at == target, 1.0, 0.0).astype(bf16)

        for e in range(2):
            for j in range(nz):
                base = ((z + j) % nz) * plane + e
                ranks = score[0, pl.ds(base, nd, 2), :]
                weights = score[1, pl.ds(base, nd, 2), :]
                for p in range(cap):
                    at_row = (j * cap + p) * nd
                    turned[at_row:at_row + nd, :] = jnp.where(ranks == p, weights, 0.0)
            for a in range(nz * nd * cap // LANES):
                block = slice(a * LANES, (a + 1) * LANES)
                cmb[e, :, block] = turned[block, :].T.astype(bf16)

    def shards_in_plane():
        wait(shards.at[:, pl.ds(1, nz - 1), d], sz_recv)
        mine = shards.at[:, :, d]
        for r in range(1, nx):
            send(mine, mine, sx_send.at[r - 1], sx_recv.at[r - 1], (z * nd + ((x + r) % nx) * NC + core, y))
        send(mine, mine, sc_send.at[0], sc_recv.at[0], (z * nd + x * NC + 1 - core, y))

    def shards_in_chip():
        for r in range(1, nx):
            block = shards.at[:, :, d_of(r, core)]
            wait(block, sx_recv.at[r - 1])
            send(block, block, sc_send.at[r], sc_recv.at[r], (z * nd + x * NC + 1 - core, y))

    rp = shard_ref.shape[1]
    rs = quarter * NY // (nz * nd)
    per_quarter = quarter // rs
    run = min(per_quarter, nd)

    def spread_matrix():
        into = lax.broadcasted_iota(jnp.int32, spread.shape, 1)
        at = lax.broadcasted_iota(jnp.int32, spread.shape, 0)
        inner = into % rp
        spread[...] = jnp.where((inner < rs) & (at == into // rp * rs + inner), 1.0, 0.0).astype(bf16)

    def block_of(m, q, i):
        first = q * per_quarter + i * run
        zr = (z + nz - first // nd) % nz
        return shards[m, zr, pl.ds(first % nd, run)].reshape(run * rp, hid)

    def shared_expert():
        for r in range(nx):
            wait(shards.at[:, :, d_of(r, 1 - core)], sc_recv.at[r])
        s_gate = jnp.zeros((tok, hid), f32)
        s_upper = jnp.zeros((tok, hid), f32)
        for slot, q in ((0, y), (1, left), (2, right), (3, across)):
            if slot:
                wait(tokens_y.at[slot - 1], t_recv.at[slot - 1])
            source = tokens_y[slot - 1] if slot else tokens_ref[...]
            padded[...] = jnp.dot(source, spread[...], preferred_element_type=f32).astype(bf16)
            for i in range(per_quarter // run):
                lhs = padded[:, i * run * rp:(i + 1) * run * rp]
                s_gate = s_gate + jnp.dot(lhs, block_of(0, q, i), preferred_element_type=f32)
                s_upper = s_upper + jnp.dot(lhs, block_of(1, q, i), preferred_element_type=f32)
        act = (s_gate / (1.0 + jnp.exp(-s_gate)) * s_upper).astype(bf16)
        across_rows = (((1,), (1,)), ((), ()))
        for slot, q in ((1, right), (2, left), (3, across), (0, y)):
            for i in range(per_quarter // run):
                padded[:, i * run * rp:(i + 1) * run * rp] = lax.dot_general(
                    act, block_of(2, q, i), across_rows, preferred_element_type=f32
                ).astype(bf16)
            pieces[slot] = lax.dot_general(
                padded[...], spread[...], across_rows, preferred_element_type=f32
            ).astype(bf16)
            if slot:
                send(pieces.at[slot], pieces_y.at[slot - 1], p_send.at[slot - 1], p_recv.at[slot - 1], y_peer(q))

    load_g.wait()
    load_u.wait()

    lag_b, lag_c, lag_d = 1, 2, 4

    def at_step(i, n, *calls):
        @pl.when(i == n)
        def _():
            for call in calls:
                call()

    def all_chunks(stage, e):
        def one(k, carry):
            stage(e, k)
            return carry

        lax.fori_loop(0, chunks, one, 0)

    def finish_first():
        load_d.wait()
        for slot in (1, 2, 3):
            wait(wd.at[slot], wd_recv.at[slot - 1])
        hidden_in(0)
        all_chunks(stage_e, 0)

    ready = chunks - 1 + lag_d

    def step(i, carry):
        @pl.when(i < units)
        def _():
            stage_a(i)

        @pl.when((i >= lag_b) & (i < units + lag_b))
        def _():
            stage_b(i - lag_b)

        at_step(i, 2, build_return)
        at_step(i, 4, spread_matrix)
        at_step(i, 5, shards_in_plane)
        at_step(i, 9, shards_in_chip)

        @pl.when((i >= lag_c) & (i < units + lag_c))
        def _():
            stage_c(i - lag_c)

        @pl.when(i >= lag_d)
        def _():
            stage_d(i - lag_d)

        at_step(i, ready, lambda: hidden_out(0))
        at_step(i, ready + 1, lambda: hidden_on(0))
        at_step(i, ready + 2, finish_first)
        at_step(i, ready + 3, shared_expert)
        at_step(i, ready + 4, lambda: all_chunks(stage_f, 0))
        return carry

    lax.fori_loop(0, units + lag_d, step, 0)

    hidden_out(1)
    hidden_on(1)
    hidden_in(1)

    lag_f, lag_g = 1, 3

    def step_back(i, carry):
        @pl.when(i < chunks)
        def _():
            stage_e(1, i)

        @pl.when((i >= lag_f) & (i < chunks + lag_f))
        def _():
            stage_f(1, i - lag_f)

        @pl.when(i >= lag_g)
        def _():
            stage_g(i - lag_g)

        return carry

    lax.fori_loop(0, chunks + lag_g, step_back, 0)

    wait(meta.at[:, pl.ds(tok, (nz - 1) * tok)], meta_send)
    wait(shards.at[:, pl.ds(1, nz - 1), d], sz_send)
    for r in range(nx):
        if r:
            wait(shards.at[:, :, d], sx_send.at[r - 1])
        wait(shards.at[:, :, d_of(r, core)], sc_send.at[r])
    for slot in (1, 2, 3):
        wait(tokens_y.at[slot - 1], t_send.at[slot - 1])
        wait(pieces.at[slot], p_send.at[slot - 1])
        wait(wd.at[slot], wd_send.at[slot - 1])

    def drain(k, carry):
        wait(held.at[k, pl.ds(1, nz - 1)], z_send.at[k])
        for e in range(2):
            wait(outs.at[e, k, pl.ds(1, nd - 1)], b_send.at[e, k])
            wait(part.at[e, k, pl.ds(1, nz - 1)], h_send.at[e, k])
        return carry

    lax.fori_loop(0, chunks, drain, 0)

    def drain_units(u, carry):
        wait(packed.at[u, pl.ds(1, nd - 1)], x_send.at[u])
        wait(rows.at[0, u], y_send.at[0, u])
        wait(rows.at[0, u], y_send.at[1, u])
        wait(rows.at[1, u, first], y_send.at[2, u])
        wait(rows.at[2, u, second], y_send.at[3, u])
        return carry

    lax.fori_loop(0, units, drain_units, 0)
    for e in range(2):
        u = units + e
        wait(hidden.at[0, e], y_send.at[0, u])
        wait(hidden.at[0, e], y_send.at[1, u])
        wait(hidden.at[1, e, low], y_send.at[2, u])
        wait(hidden.at[2, e, high], y_send.at[3, u])


def layer(tokens, expert_ids, gate_weights, w_gate, w_up, w_down, shard, cap):
    nz, nx = dims_of(lax.axis_size("exp"))
    nd = nx * NC
    tok, quarter = tokens.shape
    top = expert_ids.shape[1]
    width, hid = w_gate.shape[1:]
    chunks = quarter // LANES
    grp = nz * cap
    f32, bf16 = jnp.float32, jnp.bfloat16
    dma = pltpu.SemaphoreType.DMA
    vm = pltpu.VMEM
    slots = 2 * nd * grp
    rp = shard.shape[1]
    padded_cols = quarter // (width // (nz * nd)) * rp
    hbm = pl.BlockSpec(memory_space=pl.ANY)
    inside = pl.BlockSpec(memory_space=pltpu.VMEM)
    return pl.pallas_call(
        functools.partial(layer_kernel, nz, nd, cap, tok, top, chunks, hid),
        out_shape=jax.ShapeDtypeStruct((tok, quarter), bf16),
        in_specs=[inside, inside, inside, hbm, hbm, hbm, inside],
        out_specs=inside,
        scratch_shapes=[
            vm((2, width, hid), bf16),
            vm((2, width, hid), bf16),
            vm((NY, 2, hid, quarter), bf16),
            vm((2, 2 * nz * nd, tok), f32),
            vm((2 * nd, nz * tok), f32),
            vm((2, nd, grp, nz * tok), bf16),
            vm((2, tok, nz * nd * cap), bf16),
            vm((nd * grp, nd * grp), bf16),
            vm((chunks, nz, tok, LANES), bf16),
            vm((2 * chunks, nd, grp, LANES), bf16),
            vm((NY, 2 * chunks, nd, grp, LANES), bf16),
            vm((2, 2, nd // 2 * grp, hid), f32),
            vm((2, 2, nd // 2 * grp, hid), f32),
            vm((NY, 2, nd * grp, hid), bf16),
            vm((2, chunks, nd, grp, LANES), bf16),
            vm((2, chunks, nd, grp, LANES), bf16),
            vm((2, chunks, nz, nd * cap, LANES), bf16),
            vm((2, chunks, nz, nd * cap, LANES), bf16),
            vm((nz * nd * cap, tok), f32),
            vm((quarter, padded_cols), bf16),
            vm((3, nz, nd, rp, hid), bf16),
            vm((NY - 1, tok, quarter), bf16),
            vm((tok, padded_cols), bf16),
            vm((NY, tok, quarter), bf16),
            vm((NY - 1, tok, quarter), bf16),
            dma((3,)), dma((3,)), dma((3,)), dma, dma,
            dma((chunks,)), dma((chunks,)), dma((2 * chunks,)), dma((2 * chunks,)),
            dma((4, 2 * chunks + 2)), dma((4, 2 * chunks + 2)),
            dma((2, chunks)), dma((2, chunks)), dma((2, chunks)), dma((2, chunks)),
            dma, dma, dma((max(1, nx - 1),)), dma((max(1, nx - 1),)), dma((nx,)), dma((nx,)),
            dma((3,)), dma((3,)), dma((3,)), dma((3,)),
        ],
        compiler_params=pltpu.CompilerParams(
            collective_id=0, has_side_effects=True, vmem_limit_bytes=60 * 1024 * 1024
        ),
        cost_estimate=pl.CostEstimate(
            flops=2 * slots * width * hid * 3, bytes_accessed=6 * width * hid * 2, transcendentals=slots * hid
        ),
        name="layer",
    )(tokens, expert_ids.T, gate_weights.T, w_gate, w_up, w_down, shard)


def body(tokens, expert_ids, gate_weights, w_gate, w_up, w_down, s_gate, s_up, s_down):
    exp_count = lax.axis_size("exp")
    tok_count, top_count = expert_ids.shape
    experts = w_gate.shape[0] * exp_count
    capacity = max(2, 5 * tok_count * top_count // (4 * experts))
    rows = s_gate.shape[0]
    shard = jnp.stack([s_gate, s_up, s_down.T])
    shard = jnp.pad(shard, ((0, 0), (0, -rows % 64), (0, 0)))
    return layer(tokens, expert_ids, gate_weights, w_gate, w_up, w_down, shard, capacity)


def solution(mesh):
    return jax.shard_map(
        body,
        mesh=mesh,
        in_specs=(
            P("exp", "tp"),
            P("exp", None),
            P("exp", None),
            P("exp", None, "tp"),
            P("exp", None, "tp"),
            P("exp", "tp", None),
            P("exp", "tp"),
            P("exp", "tp"),
            P("tp", "exp"),
        ),
        out_specs=P("exp", "tp"),
        check_vma=False,
    )
```

time: 246 us -> 238 us (0.967)
  Pallas kernels: 240 us -> 234 us
  local copies, waits for them, and re-layouts: 4.47 us -> 1.65 us
    pallas_call x1, Pallas kernels: 240 us -> 234 us  [layer(): pl.pallas_call(functools.partial(layer_kernel, nz, nd, cap, tok, top, chu...]
    unnamed x3 -> x1, local copies, waits for them, and re-layouts: 4.47 us -> 1.65 us
where the time goes in v3:
time: 238 us; the launch traced here: 237 us
  Pallas kernels  234 us (98%)
    pallas_call x1, Pallas kernels, layer(): pl.pallas_call(functools.partial(layer_kernel, nz, nd, cap, tok, top, chu...  234 us

profile of v3, /device:TPU:1, one launch (start us, length us, event | category | flops | bytes accessed | tf_op | source)
XLA Modules:
  0.0 237.4 jit_solution(17179567995813444351)
XLA Ops:
  0.0 1.4 fusion.4.shard_ref
  1.4 234.4 %layer.1 = bf16[128,896]{1,0:T(8,128)(2,1)} custom-call(bf16[128,896]{1,0:T(8,128)(2,1)} %tokens_ref.1, s32[8,128]{1,0:T(8,128)} %bitcast.10, f32[8,128]{1,0:T(8,128)} %bitcast.11, bf16[2,3584,256]{2,1,0:T(8,128)(2,1)} %wg_hbm.1, bf16[2,3584,256]{2,1,0:T(8,128)(2,1)} %wu_hbm.1, bf16[2,256,3584]{2,1,0:T(8,128)(2,1)} %wd_hbm.1, ...), custom_call_target="tpu_custom_call" | custom-call | flops 7046430720 | bytes 11010048 | tf_op jit(solution)/shard_map/layer/pallas_call | solution.py:476
  235.8 1.6 copy.11

commit v4 on v3

--- a/solution.py
+++ b/solution.py
@@ -11,6 +11,7 @@
 NY = 4
 NC = 2
 LANES = 128
+EARLY = 0
 
 
 def dims_of(exp_count):
@@ -30,6 +31,10 @@
     sz_send, sz_recv, sx_send, sx_recv, sc_send, sc_recv, t_send, t_recv, p_send, p_recv,
 ):
     quarter = chunks * LANES
+    z_ahead = 3
+    early = min(EARLY, chunks - 3)
+    late = chunks - early
+    parts = late + NY * early
     grp = nz * cap
     f32, bf16 = jnp.float32, jnp.bfloat16
     exp = lax.axis_index("exp")
@@ -107,27 +112,50 @@
     meta[:, 0:tok] = score[0, pl.ds(pl.multiple_of(z * plane, plane), plane), :]
 
     y_slots = ((1, right), (2, left), (3, across))
-    for slot, q in y_slots:
-        send(tokens_ref, tokens_y.at[slot - 1], t_send.at[slot - 1], t_recv.at[slot - 1], y_peer(q))
-
-    def send_tokens(k, carry):
+
+    def send_tokens(i, source, k):
         cols = pl.ds(pl.multiple_of(k * LANES, LANES), LANES)
         for j in range(1, nz):
-            send(tokens_ref.at[:, cols], held.at[k, j], z_send.at[k], z_recv.at[k], z_peer(j))
-        held[k, 0] = tokens_ref[:, cols]
-        return carry
-
-    lax.fori_loop(0, chunks, send_tokens, 0)
-
-    for j in range(1, nz):
-        send(shard_ref, shards.at[:, j, d], sz_send, sz_recv, z_peer(j))
-    shards[:, 0, d] = shard_ref[...]
-
-    for slot, q in y_slots:
-        send(
-            wd_hbm.at[:, :, pl.ds(pl.multiple_of(q * quarter, LANES), quarter)],
-            wd.at[slot], wd_send.at[slot - 1], wd_recv.at[slot - 1], y_peer(q),
-        )
+            send(source.at[:, cols], held.at[i, j], z_send.at[i], z_recv.at[i], z_peer(j))
+        held[i, 0] = source[:, cols]
+
+    def send_late(k):
+        send_tokens(k, tokens_ref, k)
+
+    def send_early(n):
+        if n == 0:
+            for slot in (1, 2, 3):
+                wait(tokens_y.at[slot - 1], t_recv.at[slot - 1])
+        for slot in range(NY):
+            source = tokens_y.at[slot - 1] if slot else tokens_ref
+            send_tokens(late + NY * n + slot, source, late + n)
+
+    def send_tokens_y():
+        for slot, q in y_slots:
+            send(tokens_ref, tokens_y.at[slot - 1], t_send.at[slot - 1], t_recv.at[slot - 1], y_peer(q))
+
+    def send_wd(u):
+        e = u // chunks
+        k = u % chunks
+        for slot, q in y_slots:
+            send(
+                wd_hbm.at[e, :, pl.ds(pl.multiple_of(q * quarter + k * LANES, LANES), LANES)],
+                wd.at[slot, e, :, pl.ds(pl.multiple_of(k * LANES, LANES), LANES)],
+                wd_send.at[slot - 1, e], wd_recv.at[slot - 1, e], y_peer(q),
+            )
+
+    def send_shard():
+        for j in range(1, nz):
+            send(shard_ref, shards.at[:, j, d], sz_send, sz_recv, z_peer(j))
+        shards[:, 0, d] = shard_ref[...]
+
+    send_late(0)
+    send_tokens_y()
+    for k in range(1, z_ahead):
+        send_late(k)
+    wd_first = min(4, 2 * chunks - 2 * late)
+    for u in range(wd_first):
+        send_wd(u)
 
     wait(meta.at[:, pl.ds(tok, (nz - 1) * tok)], meta_recv)
 
@@ -147,23 +175,47 @@
     upper[...] = jnp.zeros_like(upper)
     slots = nd * grp
 
-    def stage_a(u):
-        e = u // chunks
-        k = u % chunks
+    def select(e, i, slot, u):
+        packed[e, i] = jnp.dot(
+            sel[e].reshape(slots, nz * tok), held[i].reshape(nz * tok, LANES), preferred_element_type=f32
+        ).astype(bf16).reshape(nd, grp, LANES)
+        for r in range(1, nd):
+            send(packed.at[e, i, r], rows.at[slot, u, r], x_send.at[e, i], x_recv.at[e, i], d_peer(r))
+        rows[slot, u, 0] = packed[e, i, 0]
+
+    def z_in(i):
+        wait(held.at[i, pl.ds(1, nz - 1)], z_recv.at[i])
+
+    def unit(v):
+        e = v // late
+        k = v % late
+        return e, k, e * chunks + k
+
+    def stage_a(v):
+        e, k, u = unit(v)
 
         @pl.when(e == 0)
         def _():
-            wait(held.at[k, pl.ds(1, nz - 1)], z_recv.at[k])
-
-        packed[u] = jnp.dot(
-            sel[e].reshape(slots, nz * tok), held[k].reshape(nz * tok, LANES), preferred_element_type=f32
-        ).astype(bf16).reshape(nd, grp, LANES)
-        for r in range(1, nd):
-            send(packed.at[u, r], rows.at[0, u, r], x_send.at[u], x_recv.at[u], d_peer(r))
-        rows[0, u, 0] = packed[u, 0]
-
-    def stage_b(u):
-        wait(rows.at[0, u, pl.ds(1, nd - 1)], x_recv.at[u])
+            z_in(k)
+
+        select(e, k, 0, u)
+
+    def early_out(e, n):
+        for slot in range(NY):
+            i = late + NY * n + slot
+            if e == 0:
+                z_in(i)
+            select(e, i, slot, e * chunks + late + n)
+
+    def early_in(e, n):
+        u = e * chunks + late + n
+        for slot in range(NY):
+            wait(rows.at[slot, u, pl.ds(1, nd - 1)], x_recv.at[e, late + NY * n + slot])
+        accumulate(u, ((0, y), (1, left), (2, right), (3, across)))
+
+    def stage_b(v):
+        e, k, u = unit(v)
+        wait(rows.at[0, u, pl.ds(1, nd - 1)], x_recv.at[e, k])
         send(rows.at[0, u], rows.at[1, u], y_send.at[0, u], y_recv.at[0, u], y_peer(right))
         send(rows.at[0, u], rows.at[2, u], y_send.at[1, u], y_recv.at[1, u], y_peer(left))
 
@@ -188,14 +240,16 @@
 
         lax.fori_loop(0, 2, one, 0)
 
-    def stage_c(u):
+    def stage_c(v):
+        u = unit(v)[2]
         wait(rows.at[1, u], y_recv.at[0, u])
         send(rows.at[1, u, first], rows.at[3, u, first], y_send.at[2, u], y_recv.at[2, u], y_peer(right))
         wait(rows.at[2, u], y_recv.at[1, u])
         send(rows.at[2, u, second], rows.at[3, u, second], y_send.at[3, u], y_recv.at[3, u], y_peer(left))
         accumulate(u, ((0, y), (1, left), (2, right)))
 
-    def stage_d(u):
+    def stage_d(v):
+        u = unit(v)[2]
         wait(rows.at[3, u, first], y_recv.at[2, u])
         wait(rows.at[3, u, second], y_recv.at[3, u])
         accumulate(u, ((3, across),))
@@ -285,7 +339,9 @@
 
     def shards_in_plane():
         wait(shards.at[:, pl.ds(1, nz - 1), d], sz_recv)
-        mine = shards.at[:, :, d]
+
+    def send_shards(j):
+        mine = shards.at[:, j, d]
         for r in range(1, nx):
             send(mine, mine, sx_send.at[r - 1], sx_recv.at[r - 1], (z * nd + ((x + r) % nx) * NC + core, y))
         send(mine, mine, sc_send.at[0], sc_recv.at[0], (z * nd + x * NC + 1 - core, y))
@@ -318,7 +374,7 @@
         s_gate = jnp.zeros((tok, hid), f32)
         s_upper = jnp.zeros((tok, hid), f32)
         for slot, q in ((0, y), (1, left), (2, right), (3, across)):
-            if slot:
+            if slot and not early:
                 wait(tokens_y.at[slot - 1], t_recv.at[slot - 1])
             source = tokens_y[slot - 1] if slot else tokens_ref[...]
             padded[...] = jnp.dot(source, spread[...], preferred_element_type=f32).astype(bf16)
@@ -336,13 +392,15 @@
             pieces[slot] = lax.dot_general(
                 padded[...], spread[...], across_rows, preferred_element_type=f32
             ).astype(bf16)
-            if slot:
-                send(pieces.at[slot], pieces_y.at[slot - 1], p_send.at[slot - 1], p_recv.at[slot - 1], y_peer(q))
+
+    def send_pieces():
+        for slot, q in y_slots:
+            send(pieces.at[slot], pieces_y.at[slot - 1], p_send.at[slot - 1], p_recv.at[slot - 1], y_peer(q))
 
     load_g.wait()
     load_u.wait()
 
-    lag_b, lag_c, lag_d = 1, 2, 4
+    lag_b, lag_c, lag_d = 1, 2, 3
 
     def at_step(i, n, *calls):
         @pl.when(i == n)
@@ -350,56 +408,75 @@
             for call in calls:
                 call()
 
-    def all_chunks(stage, e):
-        def one(k, carry):
-            stage(e, k)
-            return carry
-
-        lax.fori_loop(0, chunks, one, 0)
-
-    def finish_first():
+    def in_steps(i, low_step, high_step, call):
+        @pl.when((i >= low_step) & (i < high_step))
+        def _():
+            call(i - low_step)
+
+    def wd_in(e):
+        for slot in (1, 2, 3):
+            wait(wd.at[slot, e], wd_recv.at[slot - 1, e])
+
+    def first_ready():
         load_d.wait()
-        for slot in (1, 2, 3):
-            wait(wd.at[slot], wd_recv.at[slot - 1])
+        wd_in(0)
         hidden_in(0)
-        all_chunks(stage_e, 0)
-
-    ready = chunks - 1 + lag_d
+
+    def two(stage):
+        def call(i):
+            stage(0, 2 * i)
+
+            @pl.when(2 * i + 1 < chunks)
+            def _():
+                stage(0, 2 * i + 1)
+
+        return call
+
+    ready = late - 1 + lag_d
+    pairs = (chunks + 1) // 2
+    v_end = 2 * late
+    steps = v_end + lag_d
+    plane_step = min(6, steps - 3)
+
+    def two_shards(i):
+        for j in range(2):
+            send_shards(2 * i + j)
 
     def step(i, carry):
-        @pl.when(i < units)
-        def _():
-            stage_a(i)
-
-        @pl.when((i >= lag_b) & (i < units + lag_b))
-        def _():
-            stage_b(i - lag_b)
-
-        at_step(i, 2, build_return)
-        at_step(i, 4, spread_matrix)
-        at_step(i, 5, shards_in_plane)
-        at_step(i, 9, shards_in_chip)
-
-        @pl.when((i >= lag_c) & (i < units + lag_c))
-        def _():
-            stage_c(i - lag_c)
-
-        @pl.when(i >= lag_d)
-        def _():
-            stage_d(i - lag_d)
-
+        in_steps(i, 0, v_end, stage_a)
+        in_steps(i, lag_b, v_end + lag_b, stage_b)
+        in_steps(i, 0, late - z_ahead, lambda k: send_late(k + z_ahead))
+        in_steps(i, 0, units - wd_first, lambda u: send_wd(u + wd_first))
+        at_step(i, 0, build_return)
+        for n in range(early):
+            at_step(i, late - z_ahead + n, functools.partial(send_early, n))
+            at_step(i, ready - early + n, functools.partial(early_out, 0, n))
+            at_step(i, ready + 1 + n, functools.partial(early_out, 1, n))
+        at_step(i, 3, spread_matrix)
+        at_step(i, min(late - z_ahead + early, plane_step), send_shard)
+        at_step(i, plane_step, shards_in_plane)
+        in_steps(i, plane_step, plane_step + nz // 2, two_shards)
+        in_steps(i, lag_c, v_end + lag_c, stage_c)
+        in_steps(i, lag_d, v_end + lag_d, stage_d)
+        for n in range(early):
+            at_step(i, ready - early + n + 1, functools.partial(early_in, 0, n))
+            at_step(i, ready + 2 + n, functools.partial(early_in, 1, n))
         at_step(i, ready, lambda: hidden_out(0))
         at_step(i, ready + 1, lambda: hidden_on(0))
-        at_step(i, ready + 2, finish_first)
-        at_step(i, ready + 3, shared_expert)
-        at_step(i, ready + 4, lambda: all_chunks(stage_f, 0))
+        at_step(i, ready + 2, first_ready)
+        in_steps(i, ready + 2, ready + 2 + pairs, two(stage_e))
+        in_steps(i, ready + 2, ready + 2 + pairs, two(stage_f))
+        at_step(i, plane_step + nz // 2 + 1, shards_in_chip)
+        at_step(i, steps - 1, shared_expert)
         return carry
 
-    lax.fori_loop(0, units + lag_d, step, 0)
+    lax.fori_loop(0, steps, step, 0)
 
     hidden_out(1)
     hidden_on(1)
+    send_pieces()
     hidden_in(1)
+    wd_in(1)
 
     lag_f, lag_g = 1, 3
 
@@ -429,10 +506,18 @@
     for slot in (1, 2, 3):
         wait(tokens_y.at[slot - 1], t_send.at[slot - 1])
         wait(pieces.at[slot], p_send.at[slot - 1])
-        wait(wd.at[slot], wd_send.at[slot - 1])
+        for e in range(2):
+            wait(wd.at[slot, e], wd_send.at[slot - 1, e])
+
+    def drain_parts(i, carry):
+        wait(held.at[i, pl.ds(1, nz - 1)], z_send.at[i])
+        for e in range(2):
+            wait(packed.at[e, i, pl.ds(1, nd - 1)], x_send.at[e, i])
+        return carry
+
+    lax.fori_loop(0, parts, drain_parts, 0)
 
     def drain(k, carry):
-        wait(held.at[k, pl.ds(1, nz - 1)], z_send.at[k])
         for e in range(2):
             wait(outs.at[e, k, pl.ds(1, nd - 1)], b_send.at[e, k])
             wait(part.at[e, k, pl.ds(1, nz - 1)], h_send.at[e, k])
@@ -440,15 +525,15 @@
 
     lax.fori_loop(0, chunks, drain, 0)
 
-    def drain_units(u, carry):
-        wait(packed.at[u, pl.ds(1, nd - 1)], x_send.at[u])
+    def drain_units(v, carry):
+        u = unit(v)[2]
         wait(rows.at[0, u], y_send.at[0, u])
         wait(rows.at[0, u], y_send.at[1, u])
         wait(rows.at[1, u, first], y_send.at[2, u])
         wait(rows.at[2, u, second], y_send.at[3, u])
         return carry
 
-    lax.fori_loop(0, units, drain_units, 0)
+    lax.fori_loop(0, v_end, drain_units, 0)
     for e in range(2):
         u = units + e
         wait(hidden.at[0, e], y_send.at[0, u])
@@ -469,6 +554,8 @@
     dma = pltpu.SemaphoreType.DMA
     vm = pltpu.VMEM
     slots = 2 * nd * grp
+    early = min(EARLY, chunks - 3)
+    parts = chunks + (NY - 1) * early
     rp = shard.shape[1]
     padded_cols = quarter // (width // (nz * nd)) * rp
     hbm = pl.BlockSpec(memory_space=pl.ANY)
@@ -487,8 +574,8 @@
             vm((2, nd, grp, nz * tok), bf16),
             vm((2, tok, nz * nd * cap), bf16),
             vm((nd * grp, nd * grp), bf16),
-            vm((chunks, nz, tok, LANES), bf16),
-            vm((2 * chunks, nd, grp, LANES), bf16),
+            vm((parts, nz, tok, LANES), bf16),
+            vm((2, parts, nd, grp, LANES), bf16),
             vm((NY, 2 * chunks, nd, grp, LANES), bf16),
             vm((2, 2, nd // 2 * grp, hid), f32),
             vm((2, 2, nd // 2 * grp, hid), f32),
@@ -504,8 +591,8 @@
             vm((tok, padded_cols), bf16),
             vm((NY, tok, quarter), bf16),
             vm((NY - 1, tok, quarter), bf16),
-            dma((3,)), dma((3,)), dma((3,)), dma, dma,
-            dma((chunks,)), dma((chunks,)), dma((2 * chunks,)), dma((2 * chunks,)),
+            dma((3,)), dma((3, 2)), dma((3, 2)), dma, dma,
+            dma((parts,)), dma((parts,)), dma((2, parts)), dma((2, parts)),
             dma((4, 2 * chunks + 2)), dma((4, 2 * chunks + 2)),
             dma((2, chunks)), dma((2, chunks)), dma((2, chunks)), dma((2, chunks)),
             dma, dma, dma((max(1, nx - 1),)), dma((max(1, nx - 1),)), dma((nx,)), dma((nx,)),

time: 238 us -> 220 us (0.924)
  Pallas kernels: 234 us -> 216 us
    pallas_call x1, Pallas kernels: 234 us -> 216 us  [layer(): pl.pallas_call(functools.partial(layer_kernel, nz, nd, cap, tok, top, chu...]
where the time goes in v4:
time: 220 us; the launch traced here: 219 us
  Pallas kernels  216 us (98%)
    pallas_call x1, Pallas kernels, layer(): pl.pallas_call(functools.partial(layer_kernel, nz, nd, cap, tok, top, chu...  216 us

profile of v4, /device:TPU:1, one launch (start us, length us, event | category | flops | bytes accessed | tf_op | source)
XLA Modules:
  0.0 219.5 jit_solution(18290384198421823360)
XLA Ops:
  0.0 1.4 fusion.4.shard_ref
  1.4 216.4 %layer.1 = bf16[128,896]{1,0:T(8,128)(2,1)} custom-call(bf16[128,896]{1,0:T(8,128)(2,1)} %tokens_ref.1, s32[8,128]{1,0:T(8,128)} %bitcast.10, f32[8,128]{1,0:T(8,128)} %bitcast.11, bf16[2,3584,256]{2,1,0:T(8,128)(2,1)} %wg_hbm.1, bf16[2,3584,256]{2,1,0:T(8,128)(2,1)} %wu_hbm.1, bf16[2,256,3584]{2,1,0:T(8,128)(2,1)} %wd_hbm.1, ...), custom_call_target="tpu_custom_call" | custom-call | flops 7046430720 | bytes 11010048 | tf_op jit(solution)/shard_map/layer/pallas_call | solution.py:563
  217.8 1.6 copy.11

commit v5 on v4

--- a/solution.py
+++ b/solution.py
@@ -25,7 +25,7 @@
     out_ref,
     wg, wu, wd, score, meta, sel, cmb, order, held, packed, rows, gate, upper, hidden,
     outs, back, part, home, turned,
-    spread, shards, tokens_y, padded, pieces, pieces_y,
+    spread, shards, tokens_y, padded, pieces, pieces_y, mixed,
     load_sem, wd_send, wd_recv, meta_send, meta_recv, z_send, z_recv, x_send, x_recv,
     y_send, y_recv, b_send, b_recv, h_send, h_recv,
     sz_send, sz_recv, sx_send, sx_recv, sc_send, sc_recv, t_send, t_recv, p_send, p_recv,
@@ -141,7 +141,7 @@
             send(
                 wd_hbm.at[e, :, pl.ds(pl.multiple_of(q * quarter + k * LANES, LANES), LANES)],
                 wd.at[slot, e, :, pl.ds(pl.multiple_of(k * LANES, LANES), LANES)],
-                wd_send.at[slot - 1, e], wd_recv.at[slot - 1, e], y_peer(q),
+                wd_send.at[slot - 1, e * (1 + k)], wd_recv.at[slot - 1, e * (1 + k)], y_peer(q),
             )
 
     def send_shard():
@@ -153,7 +153,8 @@
     send_tokens_y()
     for k in range(1, z_ahead):
         send_late(k)
-    wd_first = min(4, 2 * chunks - 2 * late)
+    wd_first = min(4, chunks)
+    wd_next = 2
     for u in range(wd_first):
         send_wd(u)
 
@@ -169,7 +170,7 @@
         sel[g // nd, g % nd] = jnp.where(hit, 1.0, 0.0).astype(bf16)
         return carry
 
-    lax.fori_loop(0, 2 * nd, build, 0)
+    lax.fori_loop(0, nd, build, 0)
 
     gate[...] = jnp.zeros_like(gate)
     upper[...] = jnp.zeros_like(upper)
@@ -302,21 +303,14 @@
             send(part.at[e, k, j], home.at[e, k, j], h_send.at[e, k], h_recv.at[e, k], z_peer(nz - j))
 
     def stage_g(k):
-        @pl.when(k == 0)
-        def _():
-            for slot in (1, 2, 3):
-                wait(pieces_y.at[slot - 1], p_recv.at[slot - 1])
-
         cols = pl.ds(pl.multiple_of(k * LANES, LANES), LANES)
         total = pieces[0, :, cols].astype(f32)
-        for slot in (1, 2, 3):
-            total = total + pieces_y[slot - 1, :, cols].astype(f32)
         for e in range(2):
             wait(home.at[e, k, pl.ds(1, nz - 1)], h_recv.at[e, k])
             total = total + jnp.dot(
                 cmb[e], home[e, k].reshape(nz * nd * cap, LANES), preferred_element_type=f32
             )
-        out_ref[:, cols] = total.astype(bf16)
+        mixed[:, cols] = total
 
     def build_return():
         at = lax.broadcasted_iota(jnp.int32, (slots, slots), 0)
@@ -400,7 +394,7 @@
     load_g.wait()
     load_u.wait()
 
-    lag_b, lag_c, lag_d = 1, 2, 3
+    lag_b, lag_c, lag_d = 2, 3, 4
 
     def at_step(i, n, *calls):
         @pl.when(i == n)
@@ -413,13 +407,17 @@
         def _():
             call(i - low_step)
 
-    def wd_in(e):
+    def wd_in(e, k):
         for slot in (1, 2, 3):
-            wait(wd.at[slot, e], wd_recv.at[slot - 1, e])
+            if e == 0:
+                wait(wd.at[slot, 0], wd_recv.at[slot - 1, 0])
+            else:
+                cols = pl.ds(pl.multiple_of(k * LANES, LANES), LANES)
+                wait(wd.at[slot, 1, :, cols], wd_recv.at[slot - 1, 1 + k])
 
     def first_ready():
         load_d.wait()
-        wd_in(0)
+        wd_in(0, 0)
         hidden_in(0)
 
     def two(stage):
@@ -439,15 +437,15 @@
     plane_step = min(6, steps - 3)
 
     def two_shards(i):
-        for j in range(2):
-            send_shards(2 * i + j)
+        send_shards(i)
 
     def step(i, carry):
         in_steps(i, 0, v_end, stage_a)
         in_steps(i, lag_b, v_end + lag_b, stage_b)
         in_steps(i, 0, late - z_ahead, lambda k: send_late(k + z_ahead))
-        in_steps(i, 0, units - wd_first, lambda u: send_wd(u + wd_first))
-        at_step(i, 0, build_return)
+        in_steps(i, 0, chunks + wd_next - wd_first, lambda u: send_wd(u + wd_first))
+        at_step(i, 4, build_return)
+        at_step(i, 1, lambda: lax.fori_loop(nd, 2 * nd, build, 0))
         for n in range(early):
             at_step(i, late - z_ahead + n, functools.partial(send_early, n))
             at_step(i, ready - early + n, functools.partial(early_out, 0, n))
@@ -455,7 +453,7 @@
         at_step(i, 3, spread_matrix)
         at_step(i, min(late - z_ahead + early, plane_step), send_shard)
         at_step(i, plane_step, shards_in_plane)
-        in_steps(i, plane_step, plane_step + nz // 2, two_shards)
+        in_steps(i, plane_step, plane_step + nz, two_shards)
         in_steps(i, lag_c, v_end + lag_c, stage_c)
         in_steps(i, lag_d, v_end + lag_d, stage_d)
         for n in range(early):
@@ -465,8 +463,8 @@
         at_step(i, ready + 1, lambda: hidden_on(0))
         at_step(i, ready + 2, first_ready)
         in_steps(i, ready + 2, ready + 2 + pairs, two(stage_e))
-        in_steps(i, ready + 2, ready + 2 + pairs, two(stage_f))
-        at_step(i, plane_step + nz // 2 + 1, shards_in_chip)
+        in_steps(i, ready + 3, ready + 3 + pairs, two(stage_f))
+        at_step(i, steps - 2, shards_in_chip)
         at_step(i, steps - 1, shared_expert)
         return carry
 
@@ -474,15 +472,19 @@
 
     hidden_out(1)
     hidden_on(1)
+    for k in range(wd_next, chunks):
+        send_wd(chunks + k)
     send_pieces()
+    for k in range(2 * min(pairs, max(0, steps - ready - 3)), chunks):
+        stage_f(0, k)
     hidden_in(1)
-    wd_in(1)
 
     lag_f, lag_g = 1, 3
 
     def step_back(i, carry):
         @pl.when(i < chunks)
         def _():
+            wd_in(1, i)
             stage_e(1, i)
 
         @pl.when((i >= lag_f) & (i < chunks + lag_f))
@@ -496,6 +498,13 @@
         return carry
 
     lax.fori_loop(0, chunks + lag_g, step_back, 0)
+
+    for slot in (1, 2, 3):
+        wait(pieces_y.at[slot - 1], p_recv.at[slot - 1])
+    total = mixed[...]
+    for slot in (1, 2, 3):
+        total = total + pieces_y[slot - 1].astype(f32)
+    out_ref[...] = total.astype(bf16)
 
     wait(meta.at[:, pl.ds(tok, (nz - 1) * tok)], meta_send)
     wait(shards.at[:, pl.ds(1, nz - 1), d], sz_send)
@@ -506,8 +515,9 @@
     for slot in (1, 2, 3):
         wait(tokens_y.at[slot - 1], t_send.at[slot - 1])
         wait(pieces.at[slot], p_send.at[slot - 1])
-        for e in range(2):
-            wait(wd.at[slot, e], wd_send.at[slot - 1, e])
+        wait(wd.at[slot, 0], wd_send.at[slot - 1, 0])
+        for k in range(chunks):
+            wait(wd.at[slot, 1, :, pl.ds(k * LANES, LANES)], wd_send.at[slot - 1, 1 + k])
 
     def drain_parts(i, carry):
         wait(held.at[i, pl.ds(1, nz - 1)], z_send.at[i])
@@ -591,7 +601,8 @@
             vm((tok, padded_cols), bf16),
             vm((NY, tok, quarter), bf16),
             vm((NY - 1, tok, quarter), bf16),
-            dma((3,)), dma((3, 2)), dma((3, 2)), dma, dma,
+            vm((tok, quarter), f32),
+            dma((3,)), dma((3, chunks + 1)), dma((3, chunks + 1)), dma, dma,
             dma((parts,)), dma((parts,)), dma((2, parts)), dma((2, parts)),
             dma((4, 2 * chunks + 2)), dma((4, 2 * chunks + 2)),
             dma((2, chunks)), dma((2, chunks)), dma((2, chunks)), dma((2, chunks)),

time: 220 us -> 200 us (0.909)
  Pallas kernels: 216 us -> 197 us
    pallas_call x1, Pallas kernels: 216 us -> 197 us  [layer(): pl.pallas_call(functools.partial(layer_kernel, nz, nd, cap, tok, top, chu...]
where the time goes in v5:
time: 200 us
  Pallas kernels  197 us (98%)
    pallas_call x1, Pallas kernels, layer(): pl.pallas_call(functools.partial(layer_kernel, nz, nd, cap, tok, top, chu...  197 us

profile of v5, /device:TPU:1, one launch (start us, length us, event | category | flops | bytes accessed | tf_op | source)
XLA Modules:
  0.0 199.9 jit_solution(6197406381051563059)
XLA Ops:
  0.0 1.4 fusion.4.shard_ref
  1.4 196.8 %layer.1 = bf16[128,896]{1,0:T(8,128)(2,1)} custom-call(bf16[128,896]{1,0:T(8,128)(2,1)} %tokens_ref.1, s32[8,128]{1,0:T(8,128)} %bitcast.10, f32[8,128]{1,0:T(8,128)} %bitcast.11, bf16[2,3584,256]{2,1,0:T(8,128)(2,1)} %wg_hbm.1, bf16[2,3584,256]{2,1,0:T(8,128)(2,1)} %wu_hbm.1, bf16[2,256,3584]{2,1,0:T(8,128)(2,1)} %wd_hbm.1, ...), custom_call_target="tpu_custom_call" | custom-call | flops 7046430720 | bytes 11010048 | tf_op jit(solution)/shard_map/layer/pallas_call | solution.py:573
  198.3 1.6 copy.11

commit v6 on v5

--- a/solution.py
+++ b/solution.py
@@ -479,7 +479,7 @@
         stage_f(0, k)
     hidden_in(1)
 
-    lag_f, lag_g = 1, 3
+    lag_f, lag_g = 2, 5
 
     def step_back(i, carry):
         @pl.when(i < chunks)

time: 200 us -> 200 us (level)
  no operation moved by 1% of the time
where the time goes in v6:
time: 200 us; the launch traced here: 199 us
  Pallas kernels  196 us (98%)
    pallas_call x1, Pallas kernels, layer(): pl.pallas_call(functools.partial(layer_kernel, nz, nd, cap, tok, top, chu...  196 us

profile of v6, /device:TPU:1, one launch (start us, length us, event | category | flops | bytes accessed | tf_op | source)
XLA Modules:
  0.0 199.4 jit_solution(4199240441407658519)
XLA Ops:
  0.0 1.4 fusion.4.shard_ref
  1.4 196.4 %layer.1 = bf16[128,896]{1,0:T(8,128)(2,1)} custom-call(bf16[128,896]{1,0:T(8,128)(2,1)} %tokens_ref.1, s32[8,128]{1,0:T(8,128)} %bitcast.10, f32[8,128]{1,0:T(8,128)} %bitcast.11, bf16[2,3584,256]{2,1,0:T(8,128)(2,1)} %wg_hbm.1, bf16[2,3584,256]{2,1,0:T(8,128)(2,1)} %wu_hbm.1, bf16[2,256,3584]{2,1,0:T(8,128)(2,1)} %wd_hbm.1, ...), custom_call_target="tpu_custom_call" | custom-call | flops 7046430720 | bytes 11010048 | tf_op jit(solution)/shard_map/layer/pallas_call | solution.py:573
  197.8 1.6 copy.11
